TPU v7x, 768 devices: a whole 4x8x12 slice. The times are simulated.
768 devices in a mesh: gx: 96 (over z, y), gy: 8 (over x, core).
Axes of the slice: x: 4, y: 8, z: 12, core: 2. Of those that a mesh axis runs over, the one named last changes fastest.
Arguments:
- fine_state: float32 [1536, 5, 32, 1024], P(('gx', 'gy')), may hold values from -2 to 8, as said below
- fine_links: int32 [1536, 2, 5], P(('gx', 'gy')), may hold values from 0 to 3, as said below
- coarse_edges: float32 [768, 2, 5, 2, 1024], P(('gx', 'gy')), may hold values from -2 to 8, as said below
- flux_register: float32 [768, 2, 5, 1024], P(('gx', 'gy')), may hold values from -8 to 8
Outputs:
- fine_new: float32 [1536, 5, 32, 1024], P(('gx', 'gy'))
- coarse_faces: float32 [768, 2, 5, 1024], P(('gx', 'gy'))
Inputs may be any that keep to these rules, and one draw needn't show every extreme that they name: `fine_state`: conserved states (density, three momenta, total energy) of an ideal gas with ratio of specific heats 1.4: in every cell density and pressure lie in 1 to 2 and each velocity component in -1 to 1. `coarse_edges`: as fine_state: density and pressure 1 to 2, velocity components -1 to 1 in every cell. `fine_links`: columns: kind (0 a fine neighbour, 1 a coarse block), row offset plus one (0 to 2), column offset plus one (0 to 2, always 1 where kind is 1), slot (below 2 where kind is 0, below 1 where kind is 1), quadrant (0 to 3). The first block of every device has kind 1 on both sides, with row offset plus one 2 on its low side and 0 on its high side; the second block of every device has kind 0 on both sides, with row offset plus one 0 on its low side and 2 on its high side.
All inputs are finite; a program needn't handle non-finite values.
Results may differ from a plain program's by a relative error of at most 0.0003.
Values sent between devices are 32-bit elements; how exact they have to be, the bound alone decides.
A program may use at most 32 MiB of HBM per device.

v0:
```python
import jax
import jax.numpy as jnp
from jax import lax
from jax.sharding import PartitionSpec as P

ADIABATIC = 1.4
FINE_RATIO = 0.1
COARSE_RATIO = 0.05


def with_halo(cells, sides, width):
    for axis, dim in sides:
        count = lax.axis_size(axis)
        head = lax.slice_in_dim(cells, 0, width, axis=dim)
        tail = lax.slice_in_dim(cells, cells.shape[dim] - width, cells.shape[dim], axis=dim)
        cells = jnp.concatenate(
            [
                lax.ppermute(tail, axis, [(i, (i + 1) % count) for i in range(count)]),
                cells,
                lax.ppermute(head, axis, [((i + 1) % count, i) for i in range(count)]),
            ],
            axis=dim,
        )
    return cells


def shifted(block, axis, distance):
    devices = range(lax.axis_size(axis))
    route = [((i - distance) % len(devices), i) for i in devices]
    return lax.ppermute(block, axis, route)


def primitives(conserved):
    density = conserved[0]
    speed_x = conserved[1] / density
    speed_y = conserved[2] / density
    speed_z = conserved[3] / density
    kinetic = 0.5 * density * (speed_x * speed_x + speed_y * speed_y + speed_z * speed_z)
    pressure = (ADIABATIC - 1.0) * (conserved[4] - kinetic)
    return jnp.stack([density, speed_x, speed_y, speed_z, pressure])


def face_states(primitive):
    extent = primitive.shape[1]
    edge_values = 7.0 / 12.0 * (
        primitive[:, 1 : extent - 2] + primitive[:, 2 : extent - 1]
    ) - 1.0 / 12.0 * (primitive[:, 0 : extent - 3] + primitive[:, 3:extent])
    middle = primitive[:, 2 : extent - 2]
    lower_edge = edge_values[:, 0 : extent - 4]
    upper_edge = edge_values[:, 1 : extent - 3]
    slope_diff = upper_edge - lower_edge
    curvature = 6.0 * (middle - 0.5 * (lower_edge + upper_edge))
    sound_speed = jnp.sqrt(ADIABATIC * middle[4] / middle[0])
    reach_up = FINE_RATIO * jnp.maximum(middle[1] + sound_speed, 0.0)
    reach_down = FINE_RATIO * jnp.maximum(sound_speed - middle[1], 0.0)
    upper_state = upper_edge - 0.5 * reach_up * (
        slope_diff - (1.0 - 2.0 / 3.0 * reach_up) * curvature
    )
    lower_state = lower_edge + 0.5 * reach_down * (
        slope_diff + (1.0 - 2.0 / 3.0 * reach_down) * curvature
    )
    return (upper_state[:, :-1], lower_state[:, 1:])


def describe(state):
    density = state[0]
    speed_x = state[1]
    pressure = state[4]
    energy = pressure / (ADIABATIC - 1.0) + 0.5 * density * (
        speed_x * speed_x + state[2] * state[2] + state[3] * state[3]
    )
    conserved = jnp.stack(
        [density, density * speed_x, density * state[2], density * state[3], energy]
    )
    physical = jnp.stack(
        [
            density * speed_x,
            density * speed_x * speed_x + pressure,
            density * speed_x * state[2],
            density * speed_x * state[3],
            speed_x * (energy + pressure),
        ]
    )
    sound_speed = jnp.sqrt(ADIABATIC * pressure / density)
    return (energy, conserved, physical, sound_speed)


def hllc_flux(left_state, right_state):
    left_energy, left_cons, left_phys, left_sound = describe(left_state)
    right_energy, right_cons, right_phys, right_sound = describe(right_state)
    wave_left = jnp.minimum(left_state[1] - left_sound, right_state[1] - right_sound)
    wave_right = jnp.maximum(left_state[1] + left_sound, right_state[1] + right_sound)
    mass_left = left_state[0] * (wave_left - left_state[1])
    mass_right = right_state[0] * (wave_right - right_state[1])
    contact = (
        right_state[4] - left_state[4] + mass_left * left_state[1] - mass_right * right_state[1]
    ) / (mass_left - mass_right)

    def star_flux(state, energy, conserved, physical, mass, wave):
        factor = mass / (wave - contact)
        star = factor * jnp.stack(
            [
                jnp.ones_like(contact),
                contact,
                state[2],
                state[3],
                energy / state[0] + (contact - state[1]) * (contact + state[4] / mass),
            ]
        )
        return physical + wave * (star - conserved)

    star_left = star_flux(left_state, left_energy, left_cons, left_phys, mass_left, wave_left)
    star_right = star_flux(
        right_state, right_energy, right_cons, right_phys, mass_right, wave_right
    )
    return jnp.where(
        wave_left >= 0.0,
        left_phys,
        jnp.where(contact >= 0.0, star_left, jnp.where(wave_right > 0.0, star_right, right_phys)),
    )


def advance_block(extended):
    primitive = primitives(extended)
    upper_state, lower_state = face_states(primitive)
    flux = hllc_flux(upper_state, lower_state)
    interior = extended[:, 3:-3]
    updated = interior - FINE_RATIO * (flux[:, 1:] - flux[:, :-1])
    return (updated, jnp.stack([flux[:, 0], flux[:, -1]]))


def prolong(source, quadrant, low_side, width):
    fields = source.shape[0]
    grid = source.reshape(fields, 2, width, width)
    half = width // 2
    row_start = quadrant // 2 * half
    col_start = quadrant % 2 * half
    anchor = jnp.zeros((), jnp.int32)
    corner = lax.dynamic_slice(
        grid, (anchor, anchor, row_start, col_start), (fields, 2, half, half)
    )
    spread = jnp.repeat(jnp.repeat(corner, 2, axis=2), 2, axis=3).reshape(fields, 2, width * width)
    if low_side:
        return jnp.stack([spread[:, 1], spread[:, 0], spread[:, 0]], axis=1)
    return jnp.stack([spread[:, 0], spread[:, 0], spread[:, 1]], axis=1)


def place_patch(face_row, quadrant, width):
    fields = face_row.shape[0]
    half = width // 2
    averaged = face_row.reshape(fields, half, 2, half, 2).mean(axis=(2, 4))
    row_start = quadrant // 2 * half
    col_start = quadrant % 2 * half
    anchor = jnp.zeros((), jnp.int32)
    placed = lax.dynamic_update_slice(
        jnp.zeros((fields, width, width), jnp.float32), averaged, (anchor, row_start, col_start)
    )
    return 0.5 * placed.reshape(fields, width * width)


def shards(fine_state, fine_links, coarse_edges, flux_register):
    blocks = fine_state.shape[0]
    fields = fine_state.shape[1]
    width = fine_state.shape[2]
    coarse_blocks = coarse_edges.shape[0]
    faces = jnp.stack([fine_state[:, :, :3], fine_state[:, :, width - 3 :]], axis=1)[None, None]
    nearby = with_halo(faces, (("gx", 0), ("gy", 1)), 1)
    nearby = nearby.reshape(9 * blocks * 2, fields, 3, width * width)
    coarse_near = with_halo(coarse_edges[None], (("gx", 0),), 1)
    coarse_near = coarse_near.reshape(3 * coarse_blocks * 2, fields, 2, width * width)

    def one_block(operands):
        block, links = operands
        ghosts = []
        for which_side in (0, 1):
            link = links[which_side]
            fine_slot = (
                (link[1] * 3 + link[2]) * blocks + jnp.minimum(link[3], blocks - 1)
            ) * 2 + (1 - which_side)
            coarse_slot = (
                link[1] * coarse_blocks + jnp.minimum(link[3], coarse_blocks - 1)
            ) * 2 + (1 - which_side)
            from_fine = nearby[fine_slot]
            from_coarse = prolong(coarse_near[coarse_slot], link[4], which_side == 0, width)
            ghosts.append(jnp.where(link[0] == 1, from_coarse, from_fine))
        extended = jnp.concatenate([ghosts[0], block, ghosts[1]], axis=1)
        return advance_block(extended)

    updated, face_flux = lax.map(one_block, (fine_state, fine_links))
    links_flat = fine_links.reshape(blocks * 2, 5)
    side_index = jnp.tile(jnp.array([0, 1], jnp.int32), blocks)
    target = (
        links_flat[:, 1] * coarse_blocks + jnp.minimum(links_flat[:, 3], coarse_blocks - 1)
    ) * 2 + (1 - side_index)

    def patch_row(face_row, quadrant):
        return place_patch(face_row, quadrant, width)

    patches = jax.vmap(patch_row)(
        face_flux.reshape(blocks * 2, fields, width * width), links_flat[:, 4]
    )
    weight = (links_flat[:, 0] == 1).astype(jnp.float32)
    patches = patches.reshape(blocks * 2, fields * width * width) * weight[:, None]
    selector = (
        target[:, None] == jnp.arange(3 * coarse_blocks * 2, dtype=jnp.int32)[None, :]
    ).astype(jnp.float32)
    outgoing = jnp.dot(
        selector.T, patches, precision=lax.Precision.HIGHEST, preferred_element_type=jnp.float32
    )
    outgoing = outgoing.reshape(3, coarse_blocks, 2, fields, width * width)
    from_lower = shifted(outgoing[2], "gx", 1)
    from_upper = shifted(outgoing[0], "gx", -1)
    totals = flux_register + outgoing[1] + from_lower + from_upper
    orient = jnp.array([1.0, -1.0], jnp.float32)[None, :, None, None]
    coarse_faces = coarse_edges[:, :, :, 0] + COARSE_RATIO * orient * totals
    return (updated, coarse_faces)


def solution(mesh):
    in_specs = (
        P(("gx", "gy"), None, None, None),
        P(("gx", "gy"), None, None),
        P(("gx", "gy"), None, None, None, None),
        P(("gx", "gy"), None, None, None),
    )
    out_specs = (P(("gx", "gy"), None, None, None), P(("gx", "gy"), None, None, None))
    return jax.shard_map(shards, mesh=mesh, in_specs=in_specs, out_specs=out_specs, check_vma=False)
```

profile of v0, /device:TPU:1, one launch (start us, length us, event | category | flops | bytes accessed | tf_op | source)
XLA Modules:
  0.0 161.5 jit_solution(11345260302589664484)
XLA Ops:
  0.7 18.2 %collective-permute-start.1 = (f32[1,1,2,5,2,1024]{5,4,3,2,1,0:T(2,128)}, f32[1,1,2,5,2,1024]{5,4,3,2,1,0:T(2,128)S(1)}, u32[]{:S(2)}, u32[]{:S(2)}) collective-permute-start(f32[1,1,2,5,2,1024]{5,4,3,2,1,0:T(2,128)} %bitcast.257), channel_id=1, source_target_pairs={{8,0},{16,8},{24,16},{32,24},{40,32},{48,40},{56,48},{64,56},{72,6... | collective-permute-start | bytes 245768 | tf_op jit(solution)/shard_map/ppermute | solution.py:20
  18.8 1.9 %collective-permute-start = (f32[1,1,2,5,2,1024]{5,4,3,2,1,0:T(2,128)}, f32[1,1,2,5,2,1024]{5,4,3,2,1,0:T(2,128)S(1)}, u32[]{:S(2)}, u32[]{:S(2)}) collective-permute-start(f32[1,1,2,5,2,1024]{5,4,3,2,1,0:T(2,128)} %bitcast.258), channel_id=1, source_target_pairs={{0,8},{8,16},{16,24},{24,32},{32,40},{40,48},{48,56},{56,64},{64,7... | collective-permute-start | bytes 245768 | tf_op jit(solution)/shard_map/ppermute | solution.py:18
  20.8 1.1 fusion.45
  22.3 6.7 %collective-permute-start.3 = (f32[1,1,2,2,5,3,1024]{6,2,5,4,3,1,0:T(2,128)S(1)}, f32[1,1,2,2,5,3,1024]{6,2,5,4,3,1,0:T(2,128)S(1)}, u32[]{:S(2)}, u32[]{:S(2)}) collective-permute-start(f32[1,1,2,2,5,3,1024]{6,2,5,4,3,1,0:T(2,128)S(1)} %maximum_bitcast_fusion.1), channel_id=1, source_target_pairs={{8,0},{16,8},{24,16},{32,24},{40,32},{48,40},{56,48},{64,56},{72,6... | collective-permute-start | bytes 737288 | tf_op jit(solution)/shard_map/ppermute | solution.py:20
  29.0 1.9 %collective-permute-start.2 = (f32[1,1,2,2,5,3,1024]{6,2,5,4,3,1,0:T(2,128)S(1)}, f32[1,1,2,2,5,3,1024]{6,2,5,4,3,1,0:T(2,128)S(1)}, u32[]{:S(2)}, u32[]{:S(2)}) collective-permute-start(f32[1,1,2,2,5,3,1024]{6,2,5,4,3,1,0:T(2,128)S(1)} %maximum_bitcast_fusion.1), channel_id=1, source_target_pairs={{0,8},{8,16},{16,24},{24,32},{32,40},{40,48},{48,56},{56,64},{64,7... | collective-permute-start | bytes 737288 | tf_op jit(solution)/shard_map/ppermute | solution.py:18
  31.0 0.8 compare_select_fusion.1
  31.8 1.2 collective-permute-done.3
  32.9 7.2 %collective-permute-done.2 = f32[1,1,2,2,5,3,1024]{6,2,5,4,3,1,0:T(2,128)S(1)} collective-permute-done((f32[1,1,2,2,5,3,1024]{6,2,5,4,3,1,0:T(2,128)S(1)}, f32[1,1,2,2,5,3,1024]{6,2,5,4,3,1,0:T(2,128)S(1)}, u32[]{:S(2)}, u32[]{:S(2)}) %collective-permute-start.2) | collective-permute-done | bytes 245792 | tf_op jit(solution)/shard_map/ppermute | solution.py:18
  40.8 2.5 %collective-permute-start.5 = (f32[3,1,2,2,5,3,1024]{6,3,5,4,2,1,0:T(2,128)S(1)}, f32[3,1,2,2,5,3,1024]{6,3,5,4,2,1,0:T(2,128)}, u32[]{:S(2)}, u32[]{:S(2)}) collective-permute-start(f32[3,1,2,2,5,3,1024]{6,3,5,4,2,1,0:T(2,128)S(1)} %copy.43), channel_id=1, source_target_pairs={{1,0},{2,1},{3,2},{4,3},{5,4},{6,5},{7,6},{0,7},{9,8},{10,9},{11,1... | collective-permute-start | bytes 2211848 | tf_op jit(solution)/shard_map/ppermute | solution.py:20
  43.3 1.1 collective-permute-start.4
  45.0 4.0 %copy.40 = f32[3,1,2,5,2,1024]{3,5,4,2,0,1:T(8,128)} copy(f32[3,1,2,5,2,1024]{5,4,3,2,1,0:T(2,128)S(1)} %pad_maximum_fusion.4) | data formatting | bytes 491520 | tf_op jit(solution)/shard_map/concatenate | solution.py:16
  49.0 4.8 %collective-permute-done.5 = f32[3,1,2,2,5,3,1024]{6,3,5,4,2,1,0:T(2,128)} collective-permute-done((f32[3,1,2,2,5,3,1024]{6,3,5,4,2,1,0:T(2,128)S(1)}, f32[3,1,2,2,5,3,1024]{6,3,5,4,2,1,0:T(2,128)}, u32[]{:S(2)}, u32[]{:S(2)}) %collective-permute-start.5) | collective-permute-done | bytes 737312 | tf_op jit(solution)/shard_map/ppermute | solution.py:20
  53.8 1.5 copy.46
  55.7 1.2 pad_maximum_fusion.2
  57.0 2.8 %copy.55 = f32[3,3,2,2,5,3,1024]{6,5,4,3,2,1,0:T(4,128)} copy(f32[3,3,2,2,5,3,1024]{6,2,5,4,3,1,0:T(2,128)S(1)} %pad_maximum_fusion.2) | data formatting | bytes 4423680 | tf_op jit(solution)/shard_map/while | solution.py:189
  59.7 47.3 %while.16 = (s32[]{:T(128)}, f32[2,5,32,1024]{3,2,1,0:T(8,128)}, f32[2,2,5,1024]{3,1,2,0:T(2,128)}, f32[2,5,32,1024]{3,2,1,0:T(8,128)S(1)}, s32[2,2,5]{2,1,0:T(2...) while((s32[]{:T(128)}, f32[2,5,32,1024]{3,2,1,0:T(8,128)}, ...), condition=%wide.region_1.2_spmd, body=%wide.region_0.1_spmd.sunk | while | flops 11306074 | bytes 39816592 | solution.py:189
  59.7 0.7 fusion.55
  63.0 1.7 %constant_dynamic-slice_fusion.12 = (f32[1,5,2,1024]{1,3,2,0:T(8,128)S(1)}, f32[1,5,2,1024]{1,3,2,0:T(8,128)S(1)}) fusion(f32[6,5,2,1024]{1,3,2,0:T(8,128)} %get-tuple-element.508, s32[]{:T(128)S(6)} %select_n.217, s32[]{:T(128)S(6)} %select_n.218), kind=kLoop, calls=%fused_computation.115.clone.1 | loop fusion | bytes 163848 | tf_op jit(solution)/shard_map/while/body/eval_jaxpr/dynamic_slice | solution.py:184
  77.0 1.0 maximum_select_fusion.3
  81.0 0.7 fusion.59
  81.7 1.0 fusion.60
  83.4 0.7 fusion.55
  86.7 1.7 %constant_dynamic-slice_fusion.12 = (f32[1,5,2,1024]{1,3,2,0:T(8,128)S(1)}, f32[1,5,2,1024]{1,3,2,0:T(8,128)S(1)}) fusion(f32[6,5,2,1024]{1,3,2,0:T(8,128)} %get-tuple-element.508, s32[]{:T(128)S(6)} %select_n.217, s32[]{:T(128)S(6)} %select_n.218), kind=kLoop, calls=%fused_computation.115.clone.1 | loop fusion | bytes 163848 | tf_op jit(solution)/shard_map/while/body/eval_jaxpr/dynamic_slice | solution.py:184
  100.7 1.0 maximum_select_fusion.3
  104.6 0.7 fusion.59
  105.4 1.0 fusion.60
  107.0 1.5 copy.51
  108.5 1.8 %reduce_sum.9 = f32[4,5,16,16]{1,3,2,0:T(8,128)S(1)} reduce(f32[4,5,16,2,16,2]{1,5,4,3,2,0:T(2,128)S(1)} %bitcast.255, f32[]{:T(128)} %constant.257.clone.1), dimensions={3,5}, to_apply=%region_2.3 | reduce | flops 15360 | bytes 102404 | tf_op jit(solution)/shard_map/vmap()/reduce_sum | solution.py:151
  110.9 38.9 %while.17 = (s32[]{:T(128)}, f32[4,5,32,32]{3,2,1,0:T(8,128)S(1)}, s32[4,4]{1,0:T(4,128)S(1)}, f32[4,5,16,16]{3,2,1,0:T(8,128)S(1)}, s32[]{:T(128)}, /*index=5*/s32[4]{0:T(128)S(1)}, s32[]{:T(128)}) while((s32[]{:T(128)}, f32[4,5,32,32]{3,2,1,0:T(8,128)S(1)}, s32[4,4]{1,0:T(4,128)S(1)}, f32[4,5,16,16]{3,2,1,0:T(8,128)S(1)}, s32[]{:T(128)}, ...), condition=%wide.while_cond, body=%wide.while_body.sunk | while | flops 1309 | bytes 25807 | solution.py:155
  111.0 0.7 fusion.62
  111.6 3.3 %and_reduce_fusion.2 = pred[]{:T(512)} fusion(s32[4]{0:T(128)S(1)} %get-tuple-element.545, s32[1]{0:T(128)} %bitcast.241, s32[1]{0:T(128)} %bitcast.242, s32[1]{0:T(128)} %bitcast.243, s32[1]{0:T(128)} %bitcast.244), kind=kLoop, calls=%fused_computation.118.clone.1 | loop fusion | flops 27 | bytes 33 | tf_op jit(solution)/shard_map/vmap(vmap())/scatter
  114.9 2.6 %dynamic-slice_select_fusion.2 = f32[1,5,16,16]{3,2,1,0:T(8,128)S(1)} fusion(f32[4,5,16,16]{3,2,1,0:T(8,128)S(1)} %get-tuple-element.543, s32[]{:T(128)S(6)} %copy.114, f32[4,5,32,32]{3,2,1,0:T(8,128)S(1)} %get-tuple-element.534, s32[]{:T(128)} %bitcast.238, s32[]{:T(128)} %bitcast.239, s32[]{:T(128)} %bitcast.240, pred[]{:T(512)} %and_reduce_fusion.2), kind=kLoop, calls=%fused_computation.117.clone.1 | loop fusion | flops 1280 | bytes 15377 | tf_op jit(solution)/shard_map/vmap(vmap())/scatter
  117.5 3.9 %dynamic-update-slice.87 = f32[4,5,32,32]{3,2,1,0:T(8,128)S(1)} dynamic-update-slice(f32[4,5,32,32]{3,2,1,0:T(8,128)S(1)} %get-tuple-element.534, f32[1,5,16,16]{3,2,1,0:T(8,128)S(1)} %dynamic-slice_select_fusion.2, s32[]{:T(128)} %bitcast.238, s32[]{:T(128)} %constant.256.clone.1..sunk.1, s32[]{:T(128)} %bitcast.239, s32[]{:T(128)} %bitcast.240) | dynamic-update-slice | bytes 10244 | tf_op jit(solution)/shard_map/vmap(vmap())/scatter
  121.4 0.7 fusion.62
  122.1 3.3 %and_reduce_fusion.2 = pred[]{:T(512)} fusion(s32[4]{0:T(128)S(1)} %get-tuple-element.545, s32[1]{0:T(128)} %bitcast.241, s32[1]{0:T(128)} %bitcast.242, s32[1]{0:T(128)} %bitcast.243, s32[1]{0:T(128)} %bitcast.244), kind=kLoop, calls=%fused_computation.118.clone.1 | loop fusion | flops 27 | bytes 33 | tf_op jit(solution)/shard_map/vmap(vmap())/scatter
  125.4 2.6 %dynamic-slice_select_fusion.2 = f32[1,5,16,16]{3,2,1,0:T(8,128)S(1)} fusion(f32[4,5,16,16]{3,2,1,0:T(8,128)S(1)} %get-tuple-element.543, s32[]{:T(128)S(6)} %copy.114, f32[4,5,32,32]{3,2,1,0:T(8,128)S(1)} %get-tuple-element.534, s32[]{:T(128)} %bitcast.238, s32[]{:T(128)} %bitcast.239, s32[]{:T(128)} %bitcast.240, pred[]{:T(512)} %and_reduce_fusion.2), kind=kLoop, calls=%fused_computation.117.clone.1 | loop fusion | flops 1280 | bytes 15377 | tf_op jit(solution)/shard_map/vmap(vmap())/scatter
  128.0 2.4 %dynamic-update-slice.87 = f32[4,5,32,32]{3,2,1,0:T(8,128)S(1)} dynamic-update-slice(f32[4,5,32,32]{3,2,1,0:T(8,128)S(1)} %get-tuple-element.534, f32[1,5,16,16]{3,2,1,0:T(8,128)S(1)} %dynamic-slice_select_fusion.2, s32[]{:T(128)} %bitcast.238, s32[]{:T(128)} %constant.256.clone.1..sunk.1, s32[]{:T(128)} %bitcast.239, s32[]{:T(128)} %bitcast.240) | dynamic-update-slice | bytes 10244 | tf_op jit(solution)/shard_map/vmap(vmap())/scatter
  130.4 0.7 fusion.62
  131.1 3.3 %and_reduce_fusion.2 = pred[]{:T(512)} fusion(s32[4]{0:T(128)S(1)} %get-tuple-element.545, s32[1]{0:T(128)} %bitcast.241, s32[1]{0:T(128)} %bitcast.242, s32[1]{0:T(128)} %bitcast.243, s32[1]{0:T(128)} %bitcast.244), kind=kLoop, calls=%fused_computation.118.clone.1 | loop fusion | flops 27 | bytes 33 | tf_op jit(solution)/shard_map/vmap(vmap())/scatter
  134.4 2.6 %dynamic-slice_select_fusion.2 = f32[1,5,16,16]{3,2,1,0:T(8,128)S(1)} fusion(f32[4,5,16,16]{3,2,1,0:T(8,128)S(1)} %get-tuple-element.543, s32[]{:T(128)S(6)} %copy.114, f32[4,5,32,32]{3,2,1,0:T(8,128)S(1)} %get-tuple-element.534, s32[]{:T(128)} %bitcast.238, s32[]{:T(128)} %bitcast.239, s32[]{:T(128)} %bitcast.240, pred[]{:T(512)} %and_reduce_fusion.2), kind=kLoop, calls=%fused_computation.117.clone.1 | loop fusion | flops 1280 | bytes 15377 | tf_op jit(solution)/shard_map/vmap(vmap())/scatter
  137.0 3.8 %dynamic-update-slice.87 = f32[4,5,32,32]{3,2,1,0:T(8,128)S(1)} dynamic-update-slice(f32[4,5,32,32]{3,2,1,0:T(8,128)S(1)} %get-tuple-element.534, f32[1,5,16,16]{3,2,1,0:T(8,128)S(1)} %dynamic-slice_select_fusion.2, s32[]{:T(128)} %bitcast.238, s32[]{:T(128)} %constant.256.clone.1..sunk.1, s32[]{:T(128)} %bitcast.239, s32[]{:T(128)} %bitcast.240) | dynamic-update-slice | bytes 10244 | tf_op jit(solution)/shard_map/vmap(vmap())/scatter
  140.8 0.7 fusion.62
  141.5 3.3 %and_reduce_fusion.2 = pred[]{:T(512)} fusion(s32[4]{0:T(128)S(1)} %get-tuple-element.545, s32[1]{0:T(128)} %bitcast.241, s32[1]{0:T(128)} %bitcast.242, s32[1]{0:T(128)} %bitcast.243, s32[1]{0:T(128)} %bitcast.244), kind=kLoop, calls=%fused_computation.118.clone.1 | loop fusion | flops 27 | bytes 33 | tf_op jit(solution)/shard_map/vmap(vmap())/scatter
  144.8 2.6 %dynamic-slice_select_fusion.2 = f32[1,5,16,16]{3,2,1,0:T(8,128)S(1)} fusion(f32[4,5,16,16]{3,2,1,0:T(8,128)S(1)} %get-tuple-element.543, s32[]{:T(128)S(6)} %copy.114, f32[4,5,32,32]{3,2,1,0:T(8,128)S(1)} %get-tuple-element.534, s32[]{:T(128)} %bitcast.238, s32[]{:T(128)} %bitcast.239, s32[]{:T(128)} %bitcast.240, pred[]{:T(512)} %and_reduce_fusion.2), kind=kLoop, calls=%fused_computation.117.clone.1 | loop fusion | flops 1280 | bytes 15377 | tf_op jit(solution)/shard_map/vmap(vmap())/scatter
  147.3 2.5 %dynamic-update-slice.87 = f32[4,5,32,32]{3,2,1,0:T(8,128)S(1)} dynamic-update-slice(f32[4,5,32,32]{3,2,1,0:T(8,128)S(1)} %get-tuple-element.534, f32[1,5,16,16]{3,2,1,0:T(8,128)S(1)} %dynamic-slice_select_fusion.2, s32[]{:T(128)} %bitcast.238, s32[]{:T(128)} %constant.256.clone.1..sunk.1, s32[]{:T(128)} %bitcast.239, s32[]{:T(128)} %bitcast.240) | dynamic-update-slice | bytes 10244 | tf_op jit(solution)/shard_map/vmap(vmap())/scatter
  150.5 1.9 %collective-permute-start.7 = (f32[1,2,5,1024]{3,2,1,0:T(8,128)S(1)}, f32[1,2,5,1024]{3,2,1,0:T(8,128)S(1)}, u32[]{:S(2)}, u32[]{:S(2)}) collective-permute-start(f32[1,2,5,1024]{3,2,1,0:T(8,128)S(1)} %squeeze.212), channel_id=1, source_target_pairs={{8,0},{16,8},{24,16},{32,24},{40,32},{48,40},{56,48},{64,56},{72,6... | collective-permute-start | bytes 122888 | tf_op jit(solution)/shard_map/ppermute | solution.py:30
  152.4 3.4 %collective-permute-start.6 = (f32[1,2,5,1024]{3,2,1,0:T(8,128)S(1)}, f32[1,2,5,1024]{3,2,1,0:T(8,128)S(1)}, u32[]{:S(2)}, u32[]{:S(2)}) collective-permute-start(f32[1,2,5,1024]{3,2,1,0:T(8,128)S(1)} %squeeze.211), channel_id=1, source_target_pairs={{760,0},{0,8},{8,16},{16,24},{24,32},{32,40},{40,48},{48,56},{56,6... | collective-permute-start | bytes 122888 | tf_op jit(solution)/shard_map/ppermute | solution.py:30
  155.9 4.9 %collective-permute-done.6 = f32[1,2,5,1024]{3,2,1,0:T(8,128)S(1)} collective-permute-done((f32[1,2,5,1024]{3,2,1,0:T(8,128)S(1)}, f32[1,2,5,1024]{3,2,1,0:T(8,128)S(1)}, u32[]{:S(2)}, u32[]{:S(2)}) %collective-permute-start.6) | collective-permute-done | bytes 40992 | tf_op jit(solution)/shard_map/ppermute | solution.py:30
  (143 shorter events, 15.6 us)
Async XLA Ops:
  0.6 43.8 %copy-start.2 = (s32[2,2,5]{2,1,0:T(2,128)S(1)}, s32[2,2,5]{2,1,0:T(2,128)}, u32[]{:S(2)}) copy-start(s32[2,2,5]{2,1,0:T(2,128)} %param.9) | copy-start | bytes 244
  0.6 44.1 %copy-start.6 = (s32[3]{0:T(128)S(1)}, s32[3]{0:T(128)}, u32[]{:S(2)}) copy-start(s32[3]{0:T(128)} %constant.264.clone.1) | copy-start | bytes 40
  0.7 44.2 %copy-start.1 = (f32[1,2,5,2,1024]{4,3,2,1,0:T(2,128)S(1)}, f32[1,2,5,2,1024]{4,3,2,1,0:T(2,128)}, u32[]{:S(2)}) copy-start(f32[1,2,5,2,1024]{4,3,2,1,0:T(2,128)} %param.10) | copy-start | bytes 245764
  0.7 44.2 %collective-permute-start.1 = (f32[1,1,2,5,2,1024]{5,4,3,2,1,0:T(2,128)}, f32[1,1,2,5,2,1024]{5,4,3,2,1,0:T(2,128)S(1)}, u32[]{:S(2)}, u32[]{:S(2)}) collective-permute-start(f32[1,1,2,5,2,1024]{5,4,3,2,1,0:T(2,128)} %bitcast.257), channel_id=1, source_target_pairs={{8,0},{16,8},{24,16},{32,24},{40,32},{48,40},{56,48},{64,56},{72,6... | collective-permute-start | bytes 245768 | tf_op jit(solution)/shard_map/ppermute | solution.py:20
  18.8 26.0 %collective-permute-start = (f32[1,1,2,5,2,1024]{5,4,3,2,1,0:T(2,128)}, f32[1,1,2,5,2,1024]{5,4,3,2,1,0:T(2,128)S(1)}, u32[]{:S(2)}, u32[]{:S(2)}) collective-permute-start(f32[1,1,2,5,2,1024]{5,4,3,2,1,0:T(2,128)} %bitcast.258), channel_id=1, source_target_pairs={{0,8},{8,16},{16,24},{24,32},{32,40},{40,48},{48,56},{56,64},{64,7... | collective-permute-start | bytes 245768 | tf_op jit(solution)/shard_map/ppermute | solution.py:18
  22.3 10.7 %collective-permute-start.3 = (f32[1,1,2,2,5,3,1024]{6,2,5,4,3,1,0:T(2,128)S(1)}, f32[1,1,2,2,5,3,1024]{6,2,5,4,3,1,0:T(2,128)S(1)}, u32[]{:S(2)}, u32[]{:S(2)}) collective-permute-start(f32[1,1,2,2,5,3,1024]{6,2,5,4,3,1,0:T(2,128)S(1)} %maximum_bitcast_fusion.1), channel_id=1, source_target_pairs={{8,0},{16,8},{24,16},{32,24},{40,32},{48,40},{56,48},{64,56},{72,6... | collective-permute-start | bytes 737288 | tf_op jit(solution)/shard_map/ppermute | solution.py:20
  29.0 11.1 %collective-permute-start.2 = (f32[1,1,2,2,5,3,1024]{6,2,5,4,3,1,0:T(2,128)S(1)}, f32[1,1,2,2,5,3,1024]{6,2,5,4,3,1,0:T(2,128)S(1)}, u32[]{:S(2)}, u32[]{:S(2)}) collective-permute-start(f32[1,1,2,2,5,3,1024]{6,2,5,4,3,1,0:T(2,128)S(1)} %maximum_bitcast_fusion.1), channel_id=1, source_target_pairs={{0,8},{8,16},{16,24},{24,32},{32,40},{40,48},{48,56},{56,64},{64,7... | collective-permute-start | bytes 737288 | tf_op jit(solution)/shard_map/ppermute | solution.py:18
  40.8 13.0 %collective-permute-start.5 = (f32[3,1,2,2,5,3,1024]{6,3,5,4,2,1,0:T(2,128)S(1)}, f32[3,1,2,2,5,3,1024]{6,3,5,4,2,1,0:T(2,128)}, u32[]{:S(2)}, u32[]{:S(2)}) collective-permute-start(f32[3,1,2,2,5,3,1024]{6,3,5,4,2,1,0:T(2,128)S(1)} %copy.43), channel_id=1, source_target_pairs={{1,0},{2,1},{3,2},{4,3},{5,4},{6,5},{7,6},{0,7},{9,8},{10,9},{11,1... | collective-permute-start | bytes 2211848 | tf_op jit(solution)/shard_map/ppermute | solution.py:20
  43.3 12.0 %collective-permute-start.4 = (f32[3,1,2,2,5,3,1024]{6,3,5,4,2,1,0:T(2,128)S(1)}, f32[3,1,2,2,5,3,1024]{6,3,5,4,2,1,0:T(2,128)S(1)}, u32[]{:S(2)}, u32[]{:S(2)}) collective-permute-start(f32[3,1,2,2,5,3,1024]{6,3,5,4,2,1,0:T(2,128)S(1)} %copy.43), channel_id=1, source_target_pairs={{0,1},{1,2},{2,3},{3,4},{4,5},{5,6},{6,7},{7,0},{8,9},{9,10},{10,1... | collective-permute-start | bytes 2211848 | tf_op jit(solution)/shard_map/ppermute | solution.py:18
  56.9 2.8 %copy-start = (f32[2,5,32,1024]{3,2,1,0:T(8,128)S(1)}, f32[2,5,32,1024]{3,2,1,0:T(8,128)}, u32[]{:S(2)}) copy-start(f32[2,5,32,1024]{3,2,1,0:T(8,128)} %param.8) | copy-start | bytes 3932164
  108.5 2.4 %copy-start.4 = (s32[4]{0:T(128)S(1)}, s32[4]{0:T(128)}, u32[]{:S(2)}) copy-start(s32[4]{0:T(128)} %constant.503) | copy-start | bytes 52
  110.3 50.4 %copy-start.3 = (f32[1,2,5,1024]{3,1,2,0:T(2,128)S(1)}, f32[1,2,5,1024]{3,1,2,0:T(2,128)}, u32[]{:S(2)}) copy-start(f32[1,2,5,1024]{3,1,2,0:T(2,128)} %param.11) | copy-start | bytes 122884
  110.3 50.4 %copy-start.5 = (f32[2]{0:T(128)S(1)}, f32[2]{0:T(128)}, u32[]{:S(2)}) copy-start(f32[2]{0:T(128)} %constant.290) | copy-start | bytes 28
  150.5 5.4 %collective-permute-start.7 = (f32[1,2,5,1024]{3,2,1,0:T(8,128)S(1)}, f32[1,2,5,1024]{3,2,1,0:T(8,128)S(1)}, u32[]{:S(2)}, u32[]{:S(2)}) collective-permute-start(f32[1,2,5,1024]{3,2,1,0:T(8,128)S(1)} %squeeze.212), channel_id=1, source_target_pairs={{8,0},{16,8},{24,16},{32,24},{40,32},{48,40},{56,48},{64,56},{72,6... | collective-permute-start | bytes 122888 | tf_op jit(solution)/shard_map/ppermute | solution.py:30
  152.4 8.3 %collective-permute-start.6 = (f32[1,2,5,1024]{3,2,1,0:T(8,128)S(1)}, f32[1,2,5,1024]{3,2,1,0:T(8,128)S(1)}, u32[]{:S(2)}, u32[]{:S(2)}) collective-permute-start(f32[1,2,5,1024]{3,2,1,0:T(8,128)S(1)} %squeeze.211), channel_id=1, source_target_pairs={{760,0},{0,8},{8,16},{16,24},{24,32},{32,40},{40,48},{48,56},{56,6... | collective-permute-start | bytes 122888 | tf_op jit(solution)/shard_map/ppermute | solution.py:30
where the time goes:
time: 165 us; the launch traced here: 162 us
  other arithmetic  40.3 us (24%)
  local copies, waits for them, and re-layouts  38.6 us (23%)
  starting transfers between devices  37.5 us (23%)
  loops' own time  25.8 us (16%)
  waiting for transfers between devices  18 us (11%)
    ppermute x3, starting transfers between devices, with_halo(): lax.ppermute(head, axis, [((i + 1) % count, i) for i in range(count)])  27.3 us
    another operation x1, loops' own time, shards(): updated, face_flux = lax.map(one_block, (fine_state, fine_links))  25.6 us
    scatter x8, other arithmetic  23.5 us
    scatter x12, local copies, waits for them, and re-layouts  15.2 us
    ppermute x3, waiting for transfers between devices, with_halo(): lax.ppermute(tail, axis, [(i, (i + 1) % count) for i in range(count)])  7.16 us
    ppermute x3, waiting for transfers between devices, with_halo(): lax.ppermute(head, axis, [((i + 1) % count, i) for i in range(count)])  5.94 us
    ppermute x2, starting transfers between devices, shifted(): return lax.ppermute(block, axis, route)  5.28 us
    ppermute x3, starting transfers between devices, with_halo(): lax.ppermute(tail, axis, [(i, (i + 1) % count) for i in range(count)])  4.96 us
  transfers between devices with their start and end apart: 8, of which 4 were waited for; matrix products, arithmetic and copies ran while one was open for 6% of the time, Pallas kernels for 0%

commit v1 on v0

v1 whole, which is shorter than its diff:
```python
import jax
import jax.numpy as jnp
from jax import lax
from jax.experimental import pallas as pl
from jax.experimental.pallas import tpu as pltpu
from jax.sharding import PartitionSpec as P

MESH = pl.DeviceIdType.MESH
FIELDS = 5
ROWS, LANES = 8, 128


def plane_rows(x):
    return pl.ds((x // 8) * 64 + x % 8, ROWS, stride=8)


def load_plane(ref, block, x):
    return [ref[block, f, plane_rows(x), :] for f in range(FIELDS)]


def primitive(cell):
    rho, mx, my, mz, energy = cell
    inverse = 1.0 / rho
    u, v, w = mx * inverse, my * inverse, mz * inverse
    p = 0.4 * (energy - 0.5 * (mx * u + my * v + mz * w))
    return [rho, u, v, w, p, inverse]


def edge(w0, w1, w2, w3):
    return [
        (7.0 / 12.0) * (w1[f] + w2[f]) - (1.0 / 12.0) * (w0[f] + w3[f]) for f in range(FIELDS)
    ]


def square_root(x):
    return jnp.sqrt(x)


def states(w, low, high):
    u = w[1]
    c = square_root(1.4 * w[4] * w[5])
    up = 0.1 * jnp.maximum(u + c, 0.0)
    down = 0.1 * jnp.maximum(c - u, 0.0)
    half_up, keep_up = 0.5 * up, 1.0 - (2.0 / 3.0) * up
    half_down, keep_down = 0.5 * down, 1.0 - (2.0 / 3.0) * down
    upper, lower = [], []
    for f in range(FIELDS):
        diff = high[f] - low[f]
        curve = 6.0 * w[f] - 3.0 * (low[f] + high[f])
        upper.append(high[f] - half_up * (diff - keep_up * curve))
        lower.append(low[f] + half_down * (diff + keep_down * curve))
    return upper, lower


def hllc(left, right):
    rho_l, u_l, v_l, w_l, p_l = left
    rho_r, u_r, v_r, w_r, p_r = right
    t_l, t_r = p_l / rho_l, p_r / rho_r
    c_l, c_r = square_root(1.4 * t_l), square_root(1.4 * t_r)
    s_l = jnp.minimum(u_l - c_l, u_r - c_r)
    s_r = jnp.maximum(u_l + c_l, u_r + c_r)
    m_l, m_r = rho_l * (s_l - u_l), rho_r * (s_r - u_r)
    contact = (p_r - p_l + m_l * u_l - m_r * u_r) / (m_l - m_r)
    is_left = jnp.maximum(s_l, contact) >= 0.0

    def pick(a, b):
        return jnp.where(is_left, a, b)

    u, v, w, p, t = (pick(a, b) for a, b in zip((u_l, v_l, w_l, p_l, t_l), (u_r, v_r, w_r, p_r, t_r)))
    m, s = pick(m_l, m_r), pick(s_l, s_r)
    star = pick(-s_l, s_r) > 0.0
    speed = jnp.where(star, contact, u)
    inverse = 1.0 / (s - speed)
    mass = m * inverse * speed
    gap = speed - u
    pressure = p + m * gap
    kinetic = 0.5 * (u * u + v * v + w * w)
    return [
        mass,
        mass * speed + pressure,
        mass * v,
        mass * w,
        mass * (2.5 * t + kinetic + gap * speed) + speed * (gap * p * inverse + pressure),
    ]


def three_fluxes(w):
    a = [edge(w[i], w[i + 1], w[i + 2], w[i + 3]) for i in range(5)]
    sides = [states(w[i + 2], a[i], a[i + 1]) for i in range(4)]
    return [hllc(sides[i][0], sides[i + 1][1]) for i in range(3)]


def iotas():
    return (
        lax.broadcasted_iota(jnp.int32, (ROWS, LANES), 0),
        lax.broadcasted_iota(jnp.int32, (ROWS, LANES), 1),
    )


def prolong(value, q):
    row, lane = iotas()
    rows = (q // 2) * 4 + row // 2
    lanes = ((row % 2) * 2 + lane // 64) * 32 + (q % 2) * 16 + (lane % 32) // 2
    return jnp.take_along_axis(jnp.take_along_axis(value, rows, axis=0), lanes, axis=1)


def patch(flux, q):
    row, lane = iotas()
    total = flux + pltpu.roll(flux, LANES - 1, 1)
    total = total + pltpu.roll(total, LANES - 32, 1)
    lanes = ((lane // 32) % 2) * 64 + 2 * (lane % 16)
    rows = 2 * (row % 4) + lane // 64
    placed = jnp.take_along_axis(jnp.take_along_axis(total, lanes, axis=1), rows, axis=0)
    inside = (row // 4 == q // 2) & ((lane % 32) // 16 == q % 2)
    return jnp.where(inside, 0.125 * placed, 0.0)


def kernel(
    n_gx, n_gy, links, fine, coarse, register, out, faces_out,
    cells, own_coarse, own_register, low_faces, high_faces,
    from_below, from_above, coarse_below, coarse_above,
    flux_out, flux_below, flux_above, kept,
    local_sem, send_sem, recv_sem,
):
    gx, gy = lax.axis_index("gx"), lax.axis_index("gy")
    above = (lax.rem(gx + 1, n_gx), gy)
    below = (lax.rem(gx + n_gx - 1, n_gx), gy)
    right = (gx, lax.rem(gy + 1, n_gy))
    left = (gx, lax.rem(gy + n_gy - 1, n_gy))

    def fetch(src, dst, k):
        copy = pltpu.make_async_copy(src, dst, local_sem.at[k])
        copy.start()
        return copy

    def rows(ref, start, size):
        return ref.at[:, :, pl.ds(start, size), :]

    edges = [fetch(rows(fine, s, 64), rows(cells, s, 64), k) for k, s in enumerate((0, 192))]
    middle = fetch(rows(fine, 64, 128), rows(cells, 64, 128), 2)
    coarse_in = fetch(coarse, own_coarse, 3)
    register_in = fetch(register, own_register, 4)

    barrier = pltpu.get_barrier_semaphore()
    for device in (above, below, right, left):
        pl.semaphore_signal(barrier, inc=1, device_id=device, device_id_type=MESH)
    pl.semaphore_wait(barrier, 4)

    def send(src, dst, device, k):
        copy = pltpu.make_async_remote_copy(
            src_ref=src, dst_ref=dst, send_sem=send_sem.at[k], recv_sem=recv_sem.at[k],
            device_id=device, device_id_type=MESH,
        )
        copy.start()
        return copy

    sent = []
    coarse_up = send(coarse.at[0], coarse_below, above, 0)
    coarse_down = send(coarse.at[1], coarse_above, below, 1)

    for copy in edges:
        copy.wait()
    for b in range(2):
        for f in range(FIELDS):
            for x in range(3):
                low_faces[b, f, x] = cells[b, f, plane_rows(x), :]
                high_faces[b, f, x] = cells[b, f, plane_rows(29 + x), :]
    fine_up, fine_down = [], []
    for b in range(2):
        fine_up.append(send(high_faces.at[b], from_below.at[1, b], above, 2 + b))
        fine_down.append(send(low_faces.at[b], from_above.at[1, b], below, 4 + b))

    def block_edge(block, side, ghosts):
        if side == 0:
            inner = [load_plane(cells, block, x) for x in range(5)]
            w = [primitive(c) for c in inner]
            fluxes = three_fluxes(ghosts + w)
            targets = (0, 1)
        else:
            inner = [load_plane(cells, block, x) for x in range(27, 32)]
            w = [primitive(c) for c in inner]
            fluxes = three_fluxes(w + ghosts)
            targets = (3, 4)
        for k, i in enumerate(targets):
            for f in range(FIELDS):
                x = i if side == 0 else 27 + i
                out[block, f, plane_rows(x), :] = inner[i][f] - 0.1 * (
                    fluxes[k + 1][f] - fluxes[k][f]
                )
        return (fluxes[0], fluxes[2]) if side == 0 else (fluxes[2], fluxes[0])

    coarse_up.wait_recv()
    coarse_down.wait_recv()
    flux_sends = []
    for side in range(2):
        q = links[0, side, 4]
        source = coarse_above if side == 0 else coarse_below
        layers = [
            primitive([
                prolong(source[f, pl.ds(layer, ROWS, stride=2), :], q) for f in range(FIELDS)
            ])
            for layer in range(2)
        ]
        near, far = layers
        ghosts = [far, near, near] if side == 0 else [near, near, far]
        outer, inner = block_edge(0, side, ghosts)
        for f in range(FIELDS):
            flux_out[side, f] = patch(outer[f], q)
            kept[0, side, f] = inner[f]
        if side == 0:
            flux_sends.append(send(flux_out.at[0], flux_below, above, 14))
        else:
            flux_sends.append(send(flux_out.at[1], flux_above, below, 15))

    middle.wait()

    def bulk(block):
        first = [load_plane(cells, block, x) for x in range(6)]
        w = [primitive(c) for c in first]
        a = [edge(w[i], w[i + 1], w[i + 2], w[i + 3]) for i in range(3)]
        upper2, _ = states(w[2], a[0], a[1])
        upper3, lower3 = states(w[3], a[1], a[2])
        flux3 = hllc(upper2, lower3)
        for f in range(FIELDS):
            kept[block, 2, f] = flux3[f]

        def step(i, carry):
            w0, w1, w2, low, upper, flux = carry
            w3 = primitive(load_plane(cells, block, i + 2))
            high = edge(w0, w1, w2, w3)
            next_upper, lower = states(w1, low, high)
            next_flux = hllc(upper, lower)
            here = plane_rows(i - 1)
            for f in range(FIELDS):
                out[block, f, here, :] = cells[block, f, here, :] - 0.1 * (next_flux[f] - flux[f])
            return w1, w2, w3, high, next_upper, next_flux

        carry = (w[3], w[4], w[5], a[2], upper3, flux3)
        carry = lax.fori_loop(0, 13, lambda k, c: step(5 + 2 * k, step(4 + 2 * k, c)), carry)
        for f in range(FIELDS):
            kept[block, 3, f] = carry[5][f]

    forwards = []
    for b in range(2):
        bulk(b)
        for k, (near, ref) in enumerate(((fine_up[b], from_below), (fine_down[b], from_above))):
            near.wait_recv()
            base = 6 + 4 * b + 2 * k
            forwards.append(send(ref.at[1, b], ref.at[0, b], right, base))
            forwards.append(send(ref.at[1, b], ref.at[2, b], left, base + 1))

    for x, side, first, second in ((2, 0, 0, 2), (29, 1, 3, 1)):
        for f in range(FIELDS):
            here = plane_rows(x)
            out[0, f, here, :] = cells[0, f, here, :] - 0.1 * (
                kept[0, 2 if side == 0 else 1, f] - kept[0, 0 if side == 0 else 3, f]
            )

    coarse_in.wait()
    register_in.wait()
    for copy in flux_sends:
        copy.wait_recv()
    for t in range(2):
        sums = flux_above if t == 0 else flux_below
        factor = 0.05 if t == 0 else -0.05
        for f in range(FIELDS):
            here = pl.ds(t, ROWS, stride=2)
            faces_out[f, here, :] = own_coarse[t, f, pl.ds(0, ROWS, stride=2), :] + factor * (
                own_register[f, here, :] + sums[f]
            )

    for copy in forwards:
        copy.wait_recv()
    for side in (1, 0):
        ref = from_below if side == 0 else from_above
        column, slot = links[1, side, 2], links[1, side, 3]
        ghosts = [
            primitive([ref[column, slot, f, x] for f in range(FIELDS)]) for x in range(3)
        ]
        _, inner = block_edge(1, side, ghosts)
        x = 2 if side == 0 else 29
        here = plane_rows(x)
        for f in range(FIELDS):
            if side == 0:
                change = kept[1, 2, f] - inner[f]
            else:
                change = inner[f] - kept[1, 3, f]
            out[1, f, here, :] = cells[1, f, here, :] - 0.1 * change

    for copy in [coarse_up, coarse_down] + fine_up + fine_down + flux_sends + forwards:
        copy.wait_send()


def shards(fine_state, fine_links, coarse_edges, flux_register):
    n_gx, n_gy = lax.axis_size("gx"), lax.axis_size("gy")
    f32 = jnp.float32
    fine = fine_state.reshape(2, FIELDS, 4, 8, 8, LANES).transpose(0, 1, 2, 4, 3, 5)
    fine = fine.reshape(2, FIELDS, 256, LANES)
    coarse = coarse_edges.reshape(2, FIELDS, 2, 8, LANES).transpose(0, 1, 3, 2, 4)
    coarse = coarse.reshape(2, FIELDS, 16, LANES)
    register = flux_register.reshape(2, FIELDS, 8, LANES).transpose(1, 2, 0, 3)
    register = register.reshape(FIELDS, 16, LANES)
    plane = (ROWS, LANES)
    updated, faces = pl.pallas_call(
        lambda *refs: kernel(n_gx, n_gy, *refs),
        out_shape=[
            pltpu.VMEM((2, FIELDS, 256, LANES), f32),
            pltpu.VMEM((FIELDS, 16, LANES), f32),
        ],
        in_specs=[
            pl.BlockSpec(memory_space=pltpu.SMEM),
            pl.BlockSpec(memory_space=pltpu.HBM),
            pl.BlockSpec(memory_space=pltpu.HBM),
            pl.BlockSpec(memory_space=pltpu.HBM),
        ],
        out_specs=[pl.BlockSpec(memory_space=pltpu.VMEM)] * 2,
        scratch_shapes=[
            pltpu.VMEM((2, FIELDS, 256, LANES), f32),
            pltpu.VMEM((2, FIELDS, 16, LANES), f32),
            pltpu.VMEM((FIELDS, 16, LANES), f32),
            pltpu.VMEM((2, FIELDS, 3) + plane, f32),
            pltpu.VMEM((2, FIELDS, 3) + plane, f32),
            pltpu.VMEM((3, 2, FIELDS, 3) + plane, f32),
            pltpu.VMEM((3, 2, FIELDS, 3) + plane, f32),
            pltpu.VMEM((FIELDS, 16, LANES), f32),
            pltpu.VMEM((FIELDS, 16, LANES), f32),
            pltpu.VMEM((2, FIELDS) + plane, f32),
            pltpu.VMEM((FIELDS,) + plane, f32),
            pltpu.VMEM((FIELDS,) + plane, f32),
            pltpu.VMEM((2, 4, FIELDS) + plane, f32),
            pltpu.SemaphoreType.DMA((5,)),
            pltpu.SemaphoreType.DMA((16,)),
            pltpu.SemaphoreType.DMA((16,)),
        ],
        compiler_params=pltpu.CompilerParams(collective_id=0, has_side_effects=True),
    )(fine_links, fine, coarse, register)
    updated = updated.reshape(2, FIELDS, 4, 8, 8, LANES).transpose(0, 1, 2, 4, 3, 5)
    faces = faces.reshape(1, FIELDS, 8, 2, LANES).transpose(0, 3, 1, 2, 4)
    return (updated.reshape(2, FIELDS, 32, 1024), faces.reshape(1, 2, FIELDS, 1024))


def solution(mesh):
    in_specs = (
        P(("gx", "gy"), None, None, None),
        P(("gx", "gy"), None, None),
        P(("gx", "gy"), None, None, None, None),
        P(("gx", "gy"), None, None, None),
    )
    out_specs = (P(("gx", "gy"), None, None, None), P(("gx", "gy"), None, None, None))
    return jax.shard_map(shards, mesh=mesh, in_specs=in_specs, out_specs=out_specs, check_vma=False)
```

time: 165 us -> 32.6 us (0.20); the launches traced: 162 us -> 32.5 us
  other arithmetic: 40.3 us -> 0 us
  starting transfers between devices: 37.5 us -> 0 us
  local copies, waits for them, and re-layouts: 38.6 us -> 1.68 us
  Pallas kernels: 0 us -> 30.1 us
  loops' own time: 25.8 us -> 0 us
  waiting for transfers between devices: 18 us -> 0 us
    ppermute x8 -> x0, starting transfers between devices: 37.5 us -> none  [the longest x3 27.3 us: with_halo(): lax.ppermute(head, axis, [((i + 1) % count, i) for i in range(count)])]
    pallas_call x0 -> x1, Pallas kernels: none -> 30.1 us  [shards(): pl.pallas_call(lambda *refs: kernel(n_gx, n_gy, *refs), out_shape=[pltpu....]
    another operation x2 -> x0, loops' own time: 25.8 us -> none  [the longest x1 25.6 us: shards(): updated, face_flux = lax.map(one_block, (fine_state, fine_links))]
    scatter x9 -> x0, other arithmetic: 23.6 us -> none
    ppermute x8 -> x0, waiting for transfers between devices: 18 us -> none  [the longest x3 7.16 us: with_halo(): lax.ppermute(tail, axis, [(i, (i + 1) % count) for i in range(count)])]
    scatter x12 -> x0, local copies, waits for them, and re-layouts: 15.2 us -> none
    while x12 -> x0, local copies, waits for them, and re-layouts: 4.42 us -> none  [the longest x2 4.29 us: shards(): updated, face_flux = lax.map(one_block, (fine_state, fine_links))]
    concatenate x2 -> x0, local copies, waits for them, and re-layouts: 4.4 us -> none  [with_halo(): jnp.concatenate([lax.ppermute(tail, axis, [(i, (i + 1) % count) for i in...]
  transfers between devices with their start and end apart: 8 -> 0, of which waited for: 4 -> 0; matrix products, arithmetic and copies ran while one was open for 6% -> 0% of each run, Pallas kernels for 0% -> 0%
where the time goes in v1:
time: 32.6 us; the launch traced here: 32.5 us
  Pallas kernels  30.1 us (92%)
  local copies, waits for them, and re-layouts  1.68 us (5%)
  between operations  0.64 us (2%)
    pallas_call x1, Pallas kernels, shards(): pl.pallas_call(lambda *refs: kernel(n_gx, n_gy, *refs), out_shape=[pltpu....  30.1 us
    unnamed x2, local copies, waits for them, and re-layouts  1.68 us

profile of v1, /device:TPU:1, one launch (start us, length us, event | category | flops | bytes accessed | tf_op | source)
XLA Modules:
  0.0 32.5 jit_solution(1105422368560540177)
XLA Ops:
  0.6 30.1 %shard_map.59 = (f32[2,5,256,128]{3,2,1,0:T(8,128)S(1)}, f32[5,16,128]{2,1,0:T(8,128)S(1)}) custom-call(s32[2,2,5]{2,1,0:T(2,128)} %refs_0_.1, f32[2,5,256,128]{3,2,1,0:T(8,128)} %bitcast.27, f32[2,5,16,128]{3,2,1,0:T(8,128)} %bitcast.28, f32[5,16,128]{2,1,0:T(8,128)} %bitcast.29), custom_call_target="tpu_custom_call" | custom-call | tf_op jit(solution)/shard_map/pallas_call | solution.py:304
  30.8 1.1 %copy.11 = f32[2,5,32,1024]{3,2,1,0:T(8,128)} copy(f32[2,5,32,1024]{3,2,1,0:T(8,128)S(1)} %bitcast.25) | data formatting | bytes 2621440
  31.8 0.6 %copy.12 = f32[1,2,5,1024]{3,1,2,0:T(2,128)} copy(f32[1,2,5,1024]{3,1,2,0:T(2,128)S(1)} %bitcast.26) | data formatting | bytes 81920

commit v2 on v1

v2 whole, which is shorter than its diff:
```python
import jax
import jax.numpy as jnp
from jax import lax
from jax.experimental import pallas as pl
from jax.experimental.pallas import tpu as pltpu
from jax.sharding import PartitionSpec as P

MESH = pl.DeviceIdType.MESH
FIELDS = 5
ROWS, LANES = 8, 128


def plane_rows(x):
    return pl.ds((x // 8) * 64 + x % 8, ROWS, stride=8)


def load_plane(ref, block, x):
    return [ref[block, f, plane_rows(x), :] for f in range(FIELDS)]


def primitive(cell):
    rho, mx, my, mz, energy = cell
    inverse = 1.0 / rho
    u, v, w = mx * inverse, my * inverse, mz * inverse
    p = 0.4 * (energy - 0.5 * (mx * u + my * v + mz * w))
    return [rho, u, v, w, p, inverse]


def edge(w0, w1, w2, w3):
    return [
        (7.0 / 12.0) * (w1[f] + w2[f]) - (1.0 / 12.0) * (w0[f] + w3[f]) for f in range(FIELDS)
    ]


def square_root(x):
    return jnp.sqrt(x)


def states(w, low, high):
    u = w[1]
    c = square_root(1.4 * w[4] * w[5])
    up = 0.1 * jnp.maximum(u + c, 0.0)
    down = 0.1 * jnp.maximum(c - u, 0.0)
    half_up, keep_up = 0.5 * up, 1.0 - (2.0 / 3.0) * up
    half_down, keep_down = 0.5 * down, 1.0 - (2.0 / 3.0) * down
    upper, lower = [], []
    for f in range(FIELDS):
        diff = high[f] - low[f]
        curve = 6.0 * w[f] - 3.0 * (low[f] + high[f])
        upper.append(high[f] - half_up * (diff - keep_up * curve))
        lower.append(low[f] + half_down * (diff + keep_down * curve))
    return upper, lower


def hllc(left, right):
    rho_l, u_l, v_l, w_l, p_l = left
    rho_r, u_r, v_r, w_r, p_r = right
    t_l, t_r = p_l / rho_l, p_r / rho_r
    c_l, c_r = square_root(1.4 * t_l), square_root(1.4 * t_r)
    s_l = jnp.minimum(u_l - c_l, u_r - c_r)
    s_r = jnp.maximum(u_l + c_l, u_r + c_r)
    m_l, m_r = rho_l * (s_l - u_l), rho_r * (s_r - u_r)
    contact = (p_r - p_l + m_l * u_l - m_r * u_r) / (m_l - m_r)
    is_left = jnp.maximum(s_l, contact) >= 0.0

    def pick(a, b):
        return jnp.where(is_left, a, b)

    u, v, w, p, t = (pick(a, b) for a, b in zip((u_l, v_l, w_l, p_l, t_l), (u_r, v_r, w_r, p_r, t_r)))
    m, s = pick(m_l, m_r), pick(s_l, s_r)
    star = pick(-s_l, s_r) > 0.0
    speed = jnp.where(star, contact, u)
    inverse = 1.0 / (s - speed)
    mass = m * inverse * speed
    gap = speed - u
    pressure = p + m * gap
    kinetic = 0.5 * (u * u + v * v + w * w)
    return [
        mass,
        mass * speed + pressure,
        mass * v,
        mass * w,
        mass * (2.5 * t + kinetic + gap * speed) + speed * (gap * p * inverse + pressure),
    ]


def three_fluxes(w):
    a = [edge(w[i], w[i + 1], w[i + 2], w[i + 3]) for i in range(5)]
    sides = [states(w[i + 2], a[i], a[i + 1]) for i in range(4)]
    return [hllc(sides[i][0], sides[i + 1][1]) for i in range(3)]


def iotas():
    return (
        lax.broadcasted_iota(jnp.int32, (ROWS, LANES), 0),
        lax.broadcasted_iota(jnp.int32, (ROWS, LANES), 1),
    )


def prolong(value, q):
    row, lane = iotas()
    rows = (q // 2) * 4 + row // 2
    lanes = ((row % 2) * 2 + lane // 64) * 32 + (q % 2) * 16 + (lane % 32) // 2
    return jnp.take_along_axis(jnp.take_along_axis(value, rows, axis=0), lanes, axis=1)


def patch(flux, q):
    row, lane = iotas()
    total = flux + pltpu.roll(flux, LANES - 1, 1)
    total = total + pltpu.roll(total, LANES - 32, 1)
    lanes = ((lane // 32) % 2) * 64 + 2 * (lane % 16)
    rows = 2 * (row % 4) + lane // 64
    placed = jnp.take_along_axis(jnp.take_along_axis(total, lanes, axis=1), rows, axis=0)
    inside = (row // 4 == q // 2) & ((lane % 32) // 16 == q % 2)
    return jnp.where(inside, 0.125 * placed, 0.0)


def single_flux(w):
    a = [edge(w[i], w[i + 1], w[i + 2], w[i + 3]) for i in range(3)]
    upper, _ = states(w[2], a[0], a[1])
    _, lower = states(w[3], a[1], a[2])
    return hllc(upper, lower)


def coarse_ghosts(ref, side, q):
    near, far = (
        primitive([prolong(ref[f, pl.ds(layer, ROWS, stride=2), :], q) for f in range(FIELDS)])
        for layer in range(2)
    )
    return [far, near, near] if side == 0 else [near, near, far]


def edge_planes(cells, block, side, ghosts, store):
    planes = range(5) if side == 0 else range(27, 32)
    inner = [load_plane(cells, block, x) for x in planes]
    w = [primitive(c) for c in inner]
    fluxes = three_fluxes(ghosts + w if side == 0 else w + ghosts)
    for k, i in enumerate((0, 1) if side == 0 else (3, 4)):
        for f in range(FIELDS):
            store(f, planes[i], inner[i][f] - 0.1 * (fluxes[k + 1][f] - fluxes[k][f]))
    return (fluxes[0], fluxes[2]) if side == 0 else (fluxes[2], fluxes[0])


def bulk(cells, out, kept, block):
    first = [load_plane(cells, block, x) for x in range(6)]
    w = [primitive(c) for c in first]
    a = [edge(w[i], w[i + 1], w[i + 2], w[i + 3]) for i in range(3)]
    upper2, _ = states(w[2], a[0], a[1])
    upper3, lower3 = states(w[3], a[1], a[2])
    flux3 = hllc(upper2, lower3)
    for f in range(FIELDS):
        kept[block, 0, f] = flux3[f]

    def step(i, carry):
        w0, w1, w2, low, upper, flux = carry
        w3 = primitive(load_plane(cells, block, i + 2))
        high = edge(w0, w1, w2, w3)
        next_upper, lower = states(w1, low, high)
        next_flux = hllc(upper, lower)
        here = plane_rows(i - 1)
        for f in range(FIELDS):
            out[block, f, here, :] = cells[block, f, here, :] - 0.1 * (next_flux[f] - flux[f])
        return w1, w2, w3, high, next_upper, next_flux

    carry = (w[3], w[4], w[5], a[2], upper3, flux3)
    carry = lax.fori_loop(0, 13, lambda k, c: step(5 + 2 * k, step(4 + 2 * k, c)), carry)
    for f in range(FIELDS):
        kept[block, 1, f] = carry[5][f]


def exchange(
    n_gx, n_gy, links, fine, coarse, register,
    out, cells, from_below, from_above, kept, faces_out,
    own_coarse, own_register, low_faces, high_faces, own_q,
    coarse_below, coarse_above, low_below, high_above, q_below, q_above,
    local_sem, send_sem, recv_sem,
):
    gx, gy = lax.axis_index("gx"), lax.axis_index("gy")
    above = (lax.rem(gx + 1, n_gx), gy)
    below = (lax.rem(gx + n_gx - 1, n_gx), gy)
    right = (gx, lax.rem(gy + 1, n_gy))
    left = (gx, lax.rem(gy + n_gy - 1, n_gy))

    def fetch(src, dst, k):
        copy = pltpu.make_async_copy(src, dst, local_sem.at[k])
        copy.start()
        return copy

    def rows(ref, start, size):
        return ref.at[:, :, pl.ds(start, size), :]

    high_in = fetch(rows(fine, 192, 64), rows(cells, 192, 64), 0)
    low_in = fetch(rows(fine, 0, 64), rows(cells, 0, 64), 1)
    middle_in = fetch(rows(fine, 64, 128), rows(cells, 64, 128), 2)
    coarse_in = fetch(coarse, own_coarse, 3)
    register_in = fetch(register, own_register, 4)

    barrier = pltpu.get_barrier_semaphore()
    for device in (above, below, right, left):
        pl.semaphore_signal(barrier, inc=1, device_id=device, device_id_type=MESH)
    pl.semaphore_wait(barrier, 4)

    sent = []

    def send(src, dst, device):
        k = len(sent)
        copy = pltpu.make_async_remote_copy(
            src_ref=src, dst_ref=dst, send_sem=send_sem.at[k], recv_sem=recv_sem.at[k],
            device_id=device, device_id_type=MESH,
        )
        copy.start()
        sent.append(copy)
        return copy

    coarse_up = send(coarse.at[0], coarse_below, above)
    high_in.wait()
    for b in range(2):
        for f in range(FIELDS):
            for x in range(3):
                high_faces[b, f, x] = cells[b, f, plane_rows(29 + x), :]
    fine_up = [send(high_faces.at[b], from_below.at[1, b], above) for b in range(2)]
    low_in.wait()
    for b in range(2):
        for f in range(FIELDS):
            for x in range(3):
                low_faces[b, f, x] = cells[b, f, plane_rows(x), :]
    for side in range(2):
        own_q[side] = jnp.full((ROWS, LANES), links[0, side, 4], jnp.int32)
    low_up = send(low_faces.at[0], low_below, above)
    q_up = send(own_q.at[0], q_below, above)
    coarse_down = send(coarse.at[1], coarse_above, below)
    fine_down = [send(low_faces.at[b], from_above.at[1, b], below) for b in range(2)]
    high_down = send(high_faces.at[0], high_above, below)
    q_down = send(own_q.at[1], q_above, below)

    def forward(copies, ref):
        for b in range(2):
            copies[b].wait_recv()
            forwards.append(send(ref.at[1, b], ref.at[0, b], right))
            forwards.append(send(ref.at[1, b], ref.at[2, b], left))

    forwards = []
    forward(fine_down, from_above)
    middle_in.wait()
    bulk(cells, out, kept, 0)
    forward(fine_up, from_below)
    bulk(cells, out, kept, 1)

    def store(f, x, value):
        out[0, f, plane_rows(x), :] = value

    coarse_down.wait_recv()
    coarse_up.wait_recv()
    for side in range(2):
        ghosts = coarse_ghosts(coarse_above if side == 0 else coarse_below, side, links[0, side, 4])
        _, third = edge_planes(cells, 0, side, ghosts, store)
        x = 2 if side == 0 else 29
        for f in range(FIELDS):
            change = kept[0, 0, f] - third[f] if side == 0 else third[f] - kept[0, 1, f]
            store(f, x, cells[0, f, plane_rows(x), :] - 0.1 * change)

    coarse_in.wait()
    register_in.wait()
    for copy in (high_down, q_down, low_up, q_up):
        copy.wait_recv()
    for t in range(2):
        side = 1 - t
        q = q_below[...] if side == 0 else q_above[...]
        planes = low_below if side == 0 else high_above
        ghosts = coarse_ghosts(own_coarse.at[t], side, q)
        w = [primitive([planes[f, x] for f in range(FIELDS)]) for x in range(3)]
        flux = single_flux(ghosts + w if side == 0 else w + ghosts)
        factor = 0.05 if t == 0 else -0.05
        here = pl.ds(t, ROWS, stride=2)
        for f in range(FIELDS):
            faces_out[f, here, :] = own_coarse[t, f, pl.ds(0, ROWS, stride=2), :] + factor * (
                own_register[f, here, :] + patch(flux[f], q)
            )

    for copy in forwards:
        copy.wait_recv()
    for copy in sent:
        copy.wait_send()


def finish(
    links, done, cells, from_below, from_above, kept, faces, out, faces_out, tiles, sem,
):
    def put(src, dst, k):
        copy = pltpu.make_async_copy(src, dst, sem.at[k])
        copy.start()
        return copy

    copies = [
        put(done.at[0], out.at[0], 0),
        put(done.at[1, :, pl.ds(64, 128), :], out.at[1, :, pl.ds(64, 128), :], 1),
        put(faces, faces_out, 2),
    ]
    for side in range(2):
        base = 0 if side == 0 else 24
        ref = from_below if side == 0 else from_above

        def store(f, x, value):
            tiles[side, f, pl.ds(x - base, ROWS, stride=8), :] = value

        column, slot = links[1, side, 2], links[1, side, 3]
        ghosts = [
            primitive([ref[column, slot, f, x] for f in range(FIELDS)]) for x in range(3)
        ]
        _, third = edge_planes(cells, 1, side, ghosts, store)
        for f in range(FIELDS):
            x = 2 if side == 0 else 29
            change = kept[1, 0, f] - third[f] if side == 0 else third[f] - kept[1, 1, f]
            store(f, x, cells[1, f, plane_rows(x), :] - 0.1 * change)
            for x in range(3, 8) if side == 0 else range(24, 29):
                store(f, x, done[1, f, plane_rows(x), :])
        copies.append(put(tiles.at[side], out.at[1, :, pl.ds(192 * side, 64), :], 3 + side))
    for copy in copies:
        copy.wait()


def shards(fine_state, fine_links, coarse_edges, flux_register):
    n_gx, n_gy = lax.axis_size("gx"), lax.axis_size("gy")
    f32 = jnp.float32
    fine = fine_state.reshape(2, FIELDS, 4, 8, 8, LANES).transpose(0, 1, 2, 4, 3, 5)
    fine = fine.reshape(2, FIELDS, 256, LANES)
    coarse = coarse_edges.reshape(2, FIELDS, 2, 8, LANES).transpose(0, 1, 3, 2, 4)
    coarse = coarse.reshape(2, FIELDS, 16, LANES)
    register = flux_register.reshape(2, FIELDS, 8, LANES).transpose(1, 2, 0, 3)
    register = register.reshape(FIELDS, 16, LANES)
    plane = (ROWS, LANES)
    smem = pl.BlockSpec(memory_space=pltpu.SMEM)
    hbm = pl.BlockSpec(memory_space=pltpu.HBM)
    vmem = pl.BlockSpec(memory_space=pltpu.VMEM)
    held = pl.pallas_call(
        lambda *refs: exchange(n_gx, n_gy, *refs),
        out_shape=[
            pltpu.VMEM((2, FIELDS, 256, LANES), f32),
            pltpu.VMEM((2, FIELDS, 256, LANES), f32),
            pltpu.VMEM((3, 2, FIELDS, 3) + plane, f32),
            pltpu.VMEM((3, 2, FIELDS, 3) + plane, f32),
            pltpu.VMEM((2, 2, FIELDS) + plane, f32),
            pltpu.VMEM((FIELDS, 16, LANES), f32),
        ],
        in_specs=[smem, hbm, hbm, hbm],
        out_specs=[vmem] * 6,
        scratch_shapes=[
            pltpu.VMEM((2, FIELDS, 16, LANES), f32),
            pltpu.VMEM((FIELDS, 16, LANES), f32),
            pltpu.VMEM((2, FIELDS, 3) + plane, f32),
            pltpu.VMEM((2, FIELDS, 3) + plane, f32),
            pltpu.VMEM((2,) + plane, jnp.int32),
            pltpu.VMEM((FIELDS, 16, LANES), f32),
            pltpu.VMEM((FIELDS, 16, LANES), f32),
            pltpu.VMEM((FIELDS, 3) + plane, f32),
            pltpu.VMEM((FIELDS, 3) + plane, f32),
            pltpu.VMEM(plane, jnp.int32),
            pltpu.VMEM(plane, jnp.int32),
            pltpu.SemaphoreType.DMA((5,)),
            pltpu.SemaphoreType.DMA((18,)),
            pltpu.SemaphoreType.DMA((18,)),
        ],
        compiler_params=pltpu.CompilerParams(collective_id=0, has_side_effects=True),
    )(fine_links, fine, coarse, register)
    updated, faces = pl.pallas_call(
        finish,
        out_shape=[
            jax.ShapeDtypeStruct((2, FIELDS, 256, LANES), f32),
            jax.ShapeDtypeStruct((FIELDS, 16, LANES), f32),
        ],
        in_specs=[smem] + [vmem] * 6,
        out_specs=[hbm, hbm],
        scratch_shapes=[
            pltpu.VMEM((2, FIELDS, 64, LANES), f32),
            pltpu.SemaphoreType.DMA((5,)),
        ],
    )(fine_links, *held)
    updated = updated.reshape(2, FIELDS, 4, 8, 8, LANES).transpose(0, 1, 2, 4, 3, 5)
    faces = faces.reshape(1, FIELDS, 8, 2, LANES).transpose(0, 3, 1, 2, 4)
    return (updated.reshape(2, FIELDS, 32, 1024), faces.reshape(1, 2, FIELDS, 1024))


def solution(mesh):
    in_specs = (
        P(("gx", "gy"), None, None, None),
        P(("gx", "gy"), None, None),
        P(("gx", "gy"), None, None, None, None),
        P(("gx", "gy"), None, None, None),
    )
    out_specs = (P(("gx", "gy"), None, None, None), P(("gx", "gy"), None, None, None))
    return jax.shard_map(shards, mesh=mesh, in_specs=in_specs, out_specs=out_specs, check_vma=False)
```

time: 32.6 us -> 37.1 us (1.14)
  local copies, waits for them, and re-layouts: 1.68 us -> 4.85 us
  Pallas kernels: 30.1 us -> 31.4 us
    unnamed x2 -> x12, local copies, waits for them, and re-layouts: 1.68 us -> 4.85 us
    pallas_call x1 -> x2, Pallas kernels: 30.1 us -> 31.4 us  [the longest x1 28.4 us: shards(): pl.pallas_call(lambda *refs: exchange(n_gx, n_gy, *refs), out_shape=[pltp...]
where the time goes in v2:
time: 37.1 us; the launch traced here: 36.9 us
  Pallas kernels  31.4 us (85%)
  local copies, waits for them, and re-layouts  4.85 us (13%)
  between operations  0.65 us (2%)
    pallas_call x1, Pallas kernels, shards(): pl.pallas_call(lambda *refs: exchange(n_gx, n_gy, *refs), out_shape=[pltp...  28.4 us
    unnamed x12, local copies, waits for them, and re-layouts  4.85 us
    pallas_call x1, Pallas kernels, shards(): pl.pallas_call(finish, out_shape=[jax.ShapeDtypeStruct((2, FIELDS, 256, L...  3.01 us

profile of v2, /device:TPU:1, one launch (start us, length us, event | category | flops | bytes accessed | tf_op | source)
XLA Modules:
  0.0 36.9 jit_solution(18411342912307700068)
XLA Ops:
  0.6 28.4 %shard_map.59 = (f32[2,5,256,128]{3,2,1,0:T(8,128)S(1)}, f32[2,5,256,128]{3,2,1,0:T(8,128)S(1)}, f32[3,2,5,3,8,128]{5,4,3,2,1,0:T(8,128)S(1)}, f32[3,2,5,3,8,128...) custom-call(s32[2,2,5]{2,1,0:T(2,128)} %links.1, f32[2,5,256,128]{3,2,1,0:T(8,128)} %bitcast.25, ...), custom_call_target="tpu_custom_call" | custom-call | tf_op jit(solution)/shard_map/pallas_call | solution.py:335
  29.1 0.0 copy-start
  29.1 1.1 %copy-done = f32[2,5,256,128]{3,2,1,0:T(8,128)} copy-done((f32[2,5,256,128]{3,2,1,0:T(8,128)}, f32[2,5,256,128]{3,2,1,0:T(8,128)S(1)}, u32[]{:S(2)}) %copy-start) | copy-done | bytes 1310744
  30.1 0.0 copy-start.1
  30.1 1.1 %copy-done.1 = f32[2,5,256,128]{3,2,1,0:T(8,128)} copy-done((f32[2,5,256,128]{3,2,1,0:T(8,128)}, f32[2,5,256,128]{3,2,1,0:T(8,128)S(1)}, u32[]{:S(2)}) %copy-start.1) | copy-done | bytes 1310744
  31.2 0.0 copy-start.2
  31.2 0.7 %copy-done.2 = f32[3,2,5,3,8,128]{5,4,3,2,1,0:T(8,128)} copy-done((f32[3,2,5,3,8,128]{5,4,3,2,1,0:T(8,128)}, f32[3,2,5,3,8,128]{5,4,3,2,1,0:T(8,128)S(1)}, u32[]{:S(2)}) %copy-start.2) | copy-done | bytes 368664
  32.0 0.0 copy-start.3
  32.0 0.7 %copy-done.3 = f32[3,2,5,3,8,128]{5,4,3,2,1,0:T(8,128)} copy-done((f32[3,2,5,3,8,128]{5,4,3,2,1,0:T(8,128)}, f32[3,2,5,3,8,128]{5,4,3,2,1,0:T(8,128)S(1)}, u32[]{:S(2)}) %copy-start.3) | copy-done | bytes 368664
  32.7 0.0 copy-start.4
  32.7 0.6 %copy-done.4 = f32[2,2,5,8,128]{4,3,2,1,0:T(8,128)} copy-done((f32[2,2,5,8,128]{4,3,2,1,0:T(8,128)}, f32[2,2,5,8,128]{4,3,2,1,0:T(8,128)S(1)}, u32[]{:S(2)}) %copy-start.4) | copy-done | bytes 81944
  33.3 0.0 copy-start.5
  33.3 0.6 %copy-done.5 = f32[5,16,128]{2,1,0:T(8,128)} copy-done((f32[5,16,128]{2,1,0:T(8,128)}, f32[5,16,128]{2,1,0:T(8,128)S(1)}, u32[]{:S(2)}) %copy-start.5) | copy-done | bytes 40984
  33.9 3.0 %shard_map.60 = (f32[2,5,256,128]{3,2,1,0:T(8,128)}, f32[5,16,128]{2,1,0:T(8,128)}) custom-call(s32[2,2,5]{2,1,0:T(2,128)} %links.1, f32[2,5,256,128]{3,2,1,0:T(8,128)} %copy-done, f32[2,5,256,128]{3,2,1,0:T(8,128)} %copy-done.1, f32[3,2,5,3,8,128]{5,4,3,2,1,0:T(8,128)} %copy-done.2, f32[3,2,5,3,8,128]{5,4,3,2,1,0:T(8,128)} %copy-done.3, ...), custom_call_target="tpu_custom_call" | custom-call | tf_op jit(solution)/shard_map/pallas_call | solution.py:365
Async XLA Ops:
  29.1 1.1 %copy-start = (f32[2,5,256,128]{3,2,1,0:T(8,128)}, f32[2,5,256,128]{3,2,1,0:T(8,128)S(1)}, u32[]{:S(2)}) copy-start(f32[2,5,256,128]{3,2,1,0:T(8,128)S(1)} %get-tuple-element.10.done) | copy-start | bytes 3932164
  30.1 1.1 %copy-start.1 = (f32[2,5,256,128]{3,2,1,0:T(8,128)}, f32[2,5,256,128]{3,2,1,0:T(8,128)S(1)}, u32[]{:S(2)}) copy-start(f32[2,5,256,128]{3,2,1,0:T(8,128)S(1)} %get-tuple-element.11.cells) | copy-start | bytes 3932164
  31.2 0.7 %copy-start.2 = (f32[3,2,5,3,8,128]{5,4,3,2,1,0:T(8,128)}, f32[3,2,5,3,8,128]{5,4,3,2,1,0:T(8,128)S(1)}, u32[]{:S(2)}) copy-start(f32[3,2,5,3,8,128]{5,4,3,2,1,0:T(8,128)S(1)} %get-tuple-element.12.from_below) | copy-start | bytes 1105924
  32.0 0.7 %copy-start.3 = (f32[3,2,5,3,8,128]{5,4,3,2,1,0:T(8,128)}, f32[3,2,5,3,8,128]{5,4,3,2,1,0:T(8,128)S(1)}, u32[]{:S(2)}) copy-start(f32[3,2,5,3,8,128]{5,4,3,2,1,0:T(8,128)S(1)} %get-tuple-element.13.from_above) | copy-start | bytes 1105924
  32.7 0.6 %copy-start.4 = (f32[2,2,5,8,128]{4,3,2,1,0:T(8,128)}, f32[2,2,5,8,128]{4,3,2,1,0:T(8,128)S(1)}, u32[]{:S(2)}) copy-start(f32[2,2,5,8,128]{4,3,2,1,0:T(8,128)S(1)} %get-tuple-element.14.kept) | copy-start | bytes 245764
  33.3 0.6 %copy-start.5 = (f32[5,16,128]{2,1,0:T(8,128)}, f32[5,16,128]{2,1,0:T(8,128)S(1)}, u32[]{:S(2)}) copy-start(f32[5,16,128]{2,1,0:T(8,128)S(1)} %get-tuple-element.15.faces) | copy-start | bytes 122884

commit v3 on v2

--- a/solution.py
+++ b/solution.py
@@ -168,18 +168,29 @@
         kept[block, 1, f] = carry[5][f]
 
 
+def block_one_edge(side, ghost_planes, cells, kept, store):
+    ghosts = [primitive(plane) for plane in ghost_planes]
+    _, third = edge_planes(cells, 1, side, ghosts, store)
+    x = 2 if side == 0 else 29
+    for f in range(FIELDS):
+        change = kept[1, 0, f] - third[f] if side == 0 else third[f] - kept[1, 1, f]
+        store(f, x, cells[1, f, plane_rows(x), :] - 0.1 * change)
+
+
 def exchange(
-    n_gx, n_gy, links, fine, coarse, register,
-    out, cells, from_below, from_above, kept, faces_out,
-    own_coarse, own_register, low_faces, high_faces, own_q,
+    n_gx, n_gy, links_in, fine, coarse, register,
+    out, cells, low_ghosts, kept, faces_out,
+    from_below, from_above, links, own_coarse, own_register, low_faces, high_faces, own_q,
     coarse_below, coarse_above, low_below, high_above, q_below, q_above,
-    local_sem, send_sem, recv_sem,
+    local_sem, send_sem, recv_sem, relay_sem, beside_sem,
 ):
     gx, gy = lax.axis_index("gx"), lax.axis_index("gy")
     above = (lax.rem(gx + 1, n_gx), gy)
     below = (lax.rem(gx + n_gx - 1, n_gx), gy)
     right = (gx, lax.rem(gy + 1, n_gy))
     left = (gx, lax.rem(gy + n_gy - 1, n_gy))
+    is_first = gx == 0
+    is_last = gx == n_gx - 1
 
     def fetch(src, dst, k):
         copy = pltpu.make_async_copy(src, dst, local_sem.at[k])
@@ -189,62 +200,120 @@
     def rows(ref, start, size):
         return ref.at[:, :, pl.ds(start, size), :]
 
-    high_in = fetch(rows(fine, 192, 64), rows(cells, 192, 64), 0)
-    low_in = fetch(rows(fine, 0, 64), rows(cells, 0, 64), 1)
-    middle_in = fetch(rows(fine, 64, 128), rows(cells, 64, 128), 2)
-    coarse_in = fetch(coarse, own_coarse, 3)
-    register_in = fetch(register, own_register, 4)
+    def signal(semaphore, device):
+        pl.semaphore_signal(semaphore, inc=1, device_id=device, device_id_type=MESH)
+
+    high_in = [
+        fetch(fine.at[b, :, pl.ds(192, 64), :], cells.at[b, :, pl.ds(192, 64), :], b)
+        for b in range(2)
+    ]
 
     barrier = pltpu.get_barrier_semaphore()
-    for device in (above, below, right, left):
-        pl.semaphore_signal(barrier, inc=1, device_id=device, device_id_type=MESH)
-    pl.semaphore_wait(barrier, 4)
-
-    sent = []
-
-    def send(src, dst, device):
-        k = len(sent)
-        copy = pltpu.make_async_remote_copy(
+    signal(barrier, below)
+
+    @pl.when(jnp.logical_not(is_last))
+    def _():
+        signal(barrier, right)
+        signal(barrier, left)
+
+    low_in = fetch(rows(fine, 0, 64), rows(cells, 0, 64), 2)
+    links_in_copy = fetch(links_in, links, 3)
+    middle_in = fetch(rows(fine, 64, 128), rows(cells, 64, 128), 4)
+    coarse_in = fetch(coarse, own_coarse, 5)
+    register_in = fetch(register, own_register, 6)
+
+    pl.semaphore_wait(barrier, jnp.where(is_last, 1, 3))
+
+    def remote(src, dst, device, k):
+        return pltpu.make_async_remote_copy(
             src_ref=src, dst_ref=dst, send_sem=send_sem.at[k], recv_sem=recv_sem.at[k],
             device_id=device, device_id_type=MESH,
         )
-        copy.start()
-        sent.append(copy)
-        return copy
-
-    coarse_up = send(coarse.at[0], coarse_below, above)
-    high_in.wait()
+
+    coarse_up = remote(coarse.at[0], coarse_below, above, 0)
+    fine_up = [remote(high_faces.at[b], from_below.at[1, b], above, 1 + b) for b in range(2)]
+    low_up = remote(low_faces.at[0], low_below, above, 3)
+    q_up = remote(own_q.at[0], q_below, above, 4)
+    coarse_down = remote(coarse.at[1], coarse_above, below, 5)
+    fine_down = [remote(low_faces.at[b], from_above.at[1, b], below, 6 + b) for b in range(2)]
+    high_down = remote(high_faces.at[0], high_above, below, 8)
+    q_down = remote(own_q.at[1], q_above, below, 9)
+    on_up, on_down = (
+        [
+            [
+                remote(ref.at[1, b], ref.at[0, b], right, base + 2 * b),
+                remote(ref.at[1, b], ref.at[2, b], left, base + 2 * b + 1),
+            ]
+            for b in range(2)
+        ]
+        for ref, base in ((from_below, 10), (from_above, 14))
+    )
+
     for b in range(2):
+        high_in[b].wait()
         for f in range(FIELDS):
             for x in range(3):
                 high_faces[b, f, x] = cells[b, f, plane_rows(29 + x), :]
-    fine_up = [send(high_faces.at[b], from_below.at[1, b], above) for b in range(2)]
+        fine_up[b].start()
     low_in.wait()
     for b in range(2):
         for f in range(FIELDS):
             for x in range(3):
                 low_faces[b, f, x] = cells[b, f, plane_rows(x), :]
+    links_in_copy.wait()
     for side in range(2):
         own_q[side] = jnp.full((ROWS, LANES), links[0, side, 4], jnp.int32)
-    low_up = send(low_faces.at[0], low_below, above)
-    q_up = send(own_q.at[0], q_below, above)
-    coarse_down = send(coarse.at[1], coarse_above, below)
-    fine_down = [send(low_faces.at[b], from_above.at[1, b], below) for b in range(2)]
-    high_down = send(high_faces.at[0], high_above, below)
-    q_down = send(own_q.at[1], q_above, below)
-
-    def forward(copies, ref):
-        for b in range(2):
-            copies[b].wait_recv()
-            forwards.append(send(ref.at[1, b], ref.at[0, b], right))
-            forwards.append(send(ref.at[1, b], ref.at[2, b], left))
-
-    forwards = []
-    forward(fine_down, from_above)
     middle_in.wait()
     bulk(cells, out, kept, 0)
-    forward(fine_up, from_below)
+    for copy in fine_up:
+        copy.wait_send()
+    coarse_up.start()
+    low_up.start()
+    q_up.start()
     bulk(cells, out, kept, 1)
+
+    def forward(arriving, onward):
+        for b in range(2):
+            arriving[b].wait_recv()
+            for copy in onward[b]:
+                copy.start()
+
+    def send_down():
+        for copy in [coarse_down] + fine_down + [high_down, q_down]:
+            copy.start()
+
+    @pl.when(is_first)
+    def _():
+        forward(fine_down, on_down)
+
+    fine_up[0].wait_recv()
+
+    @pl.when(jnp.logical_not(is_first))
+    def _():
+        send_down()
+
+    @pl.when(is_last)
+    def _():
+        pl.semaphore_wait(beside_sem, 1)
+
+    for copy in on_up[0]:
+        copy.start()
+    fine_up[1].wait_recv()
+    for copy in on_up[1]:
+        copy.start()
+
+    @pl.when(is_first)
+    def _():
+        signal(relay_sem.at[0], right)
+        signal(relay_sem.at[1], left)
+        send_down()
+        pl.semaphore_wait(relay_sem.at[0], 1)
+        pl.semaphore_wait(relay_sem.at[1], 1)
+        signal(beside_sem, below)
+
+    @pl.when(jnp.logical_not(is_first))
+    def _():
+        forward(fine_down, on_down)
 
     def store(f, x, value):
         out[0, f, plane_rows(x), :] = value
@@ -258,6 +327,16 @@
         for f in range(FIELDS):
             change = kept[0, 0, f] - third[f] if side == 0 else third[f] - kept[0, 1, f]
             store(f, x, cells[0, f, plane_rows(x), :] - 0.1 * change)
+
+    def store_one(f, x, value):
+        out[1, f, plane_rows(x), :] = value
+
+    for pair in on_down:
+        for copy in pair:
+            copy.wait_recv()
+    column, slot = links[1, 1, 2], links[1, 1, 3]
+    ghost_planes = [[from_above[column, slot, f, x] for f in range(FIELDS)] for x in range(3)]
+    block_one_edge(1, ghost_planes, cells, kept, store_one)
 
     coarse_in.wait()
     register_in.wait()
@@ -277,15 +356,22 @@
                 own_register[f, here, :] + patch(flux[f], q)
             )
 
-    for copy in forwards:
-        copy.wait_recv()
-    for copy in sent:
+    for copy in [coarse_up, low_up, q_up, coarse_down, high_down, q_down] + fine_down:
         copy.wait_send()
-
-
-def finish(
-    links, done, cells, from_below, from_above, kept, faces, out, faces_out, tiles, sem,
-):
+    for pair in on_down + on_up:
+        for copy in pair:
+            copy.wait_send()
+
+    for pair in on_up:
+        for copy in pair:
+            copy.wait_recv()
+    column, slot = links[1, 0, 2], links[1, 0, 3]
+    for f in range(FIELDS):
+        for x in range(3):
+            low_ghosts[f, x] = from_below[column, slot, f, x]
+
+
+def finish(done, cells, low_ghosts, kept, faces, out, faces_out, tile, sem):
     def put(src, dst, k):
         copy = pltpu.make_async_copy(src, dst, sem.at[k])
         copy.start()
@@ -293,28 +379,19 @@
 
     copies = [
         put(done.at[0], out.at[0], 0),
-        put(done.at[1, :, pl.ds(64, 128), :], out.at[1, :, pl.ds(64, 128), :], 1),
+        put(done.at[1, :, pl.ds(64, 192), :], out.at[1, :, pl.ds(64, 192), :], 1),
         put(faces, faces_out, 2),
     ]
-    for side in range(2):
-        base = 0 if side == 0 else 24
-        ref = from_below if side == 0 else from_above
-
-        def store(f, x, value):
-            tiles[side, f, pl.ds(x - base, ROWS, stride=8), :] = value
-
-        column, slot = links[1, side, 2], links[1, side, 3]
-        ghosts = [
-            primitive([ref[column, slot, f, x] for f in range(FIELDS)]) for x in range(3)
-        ]
-        _, third = edge_planes(cells, 1, side, ghosts, store)
-        for f in range(FIELDS):
-            x = 2 if side == 0 else 29
-            change = kept[1, 0, f] - third[f] if side == 0 else third[f] - kept[1, 1, f]
-            store(f, x, cells[1, f, plane_rows(x), :] - 0.1 * change)
-            for x in range(3, 8) if side == 0 else range(24, 29):
-                store(f, x, done[1, f, plane_rows(x), :])
-        copies.append(put(tiles.at[side], out.at[1, :, pl.ds(192 * side, 64), :], 3 + side))
+
+    def store(f, x, value):
+        tile[f, pl.ds(x, ROWS, stride=8), :] = value
+
+    ghost_planes = [[low_ghosts[f, x] for f in range(FIELDS)] for x in range(3)]
+    block_one_edge(0, ghost_planes, cells, kept, store)
+    for f in range(FIELDS):
+        for x in range(3, 8):
+            store(f, x, done[1, f, plane_rows(x), :])
+    copies.append(put(tile, out.at[1, :, pl.ds(0, 64), :], 3))
     for copy in copies:
         copy.wait()
 
@@ -329,7 +406,6 @@
     register = flux_register.reshape(2, FIELDS, 8, LANES).transpose(1, 2, 0, 3)
     register = register.reshape(FIELDS, 16, LANES)
     plane = (ROWS, LANES)
-    smem = pl.BlockSpec(memory_space=pltpu.SMEM)
     hbm = pl.BlockSpec(memory_space=pltpu.HBM)
     vmem = pl.BlockSpec(memory_space=pltpu.VMEM)
     held = pl.pallas_call(
@@ -337,14 +413,16 @@
         out_shape=[
             pltpu.VMEM((2, FIELDS, 256, LANES), f32),
             pltpu.VMEM((2, FIELDS, 256, LANES), f32),
-            pltpu.VMEM((3, 2, FIELDS, 3) + plane, f32),
-            pltpu.VMEM((3, 2, FIELDS, 3) + plane, f32),
+            pltpu.VMEM((FIELDS, 3) + plane, f32),
             pltpu.VMEM((2, 2, FIELDS) + plane, f32),
             pltpu.VMEM((FIELDS, 16, LANES), f32),
         ],
-        in_specs=[smem, hbm, hbm, hbm],
-        out_specs=[vmem] * 6,
+        in_specs=[hbm] * 4,
+        out_specs=[vmem] * 5,
         scratch_shapes=[
+            pltpu.VMEM((3, 2, FIELDS, 3) + plane, f32),
+            pltpu.VMEM((3, 2, FIELDS, 3) + plane, f32),
+            pltpu.SMEM((2, 2, 5), jnp.int32),
             pltpu.VMEM((2, FIELDS, 16, LANES), f32),
             pltpu.VMEM((FIELDS, 16, LANES), f32),
             pltpu.VMEM((2, FIELDS, 3) + plane, f32),
@@ -356,9 +434,11 @@
             pltpu.VMEM((FIELDS, 3) + plane, f32),
             pltpu.VMEM(plane, jnp.int32),
             pltpu.VMEM(plane, jnp.int32),
-            pltpu.SemaphoreType.DMA((5,)),
+            pltpu.SemaphoreType.DMA((7,)),
             pltpu.SemaphoreType.DMA((18,)),
             pltpu.SemaphoreType.DMA((18,)),
+            pltpu.SemaphoreType.REGULAR((2,)),
+            pltpu.SemaphoreType.REGULAR,
         ],
         compiler_params=pltpu.CompilerParams(collective_id=0, has_side_effects=True),
     )(fine_links, fine, coarse, register)
@@ -368,13 +448,14 @@
             jax.ShapeDtypeStruct((2, FIELDS, 256, LANES), f32),
             jax.ShapeDtypeStruct((FIELDS, 16, LANES), f32),
         ],
-        in_specs=[smem] + [vmem] * 6,
+        in_specs=[vmem] * 5,
         out_specs=[hbm, hbm],
         scratch_shapes=[
-            pltpu.VMEM((2, FIELDS, 64, LANES), f32),
-            pltpu.SemaphoreType.DMA((5,)),
+            pltpu.VMEM((FIELDS, 64, LANES), f32),
+            pltpu.SemaphoreType.DMA((4,)),
         ],
-    )(fine_links, *held)
+        compiler_params=pltpu.CompilerParams(vmem_limit_bytes=8 * 2**20),
+    )(*held)
     updated = updated.reshape(2, FIELDS, 4, 8, 8, LANES).transpose(0, 1, 2, 4, 3, 5)
     faces = faces.reshape(1, FIELDS, 8, 2, LANES).transpose(0, 3, 1, 2, 4)
     return (updated.reshape(2, FIELDS, 32, 1024), faces.reshape(1, 2, FIELDS, 1024))

time: 37.1 us -> 27.7 us (0.75)
  local copies, waits for them, and re-layouts: 4.85 us -> 0 us
  Pallas kernels: 31.4 us -> 26.7 us
    unnamed x12 -> x0, local copies, waits for them, and re-layouts: 4.85 us -> none
    pallas_call x1, Pallas kernels: 28.4 us -> 25.6 us  [shards(): pl.pallas_call(lambda *refs: exchange(n_gx, n_gy, *refs), out_shape=[pltp...]
    pallas_call x1, Pallas kernels: 3.01 us -> 1.1 us  [shards(): pl.pallas_call(finish, out_shape=[jax.ShapeDtypeStruct((2, FIELDS, 256, L...]
where the time goes in v3:
time: 27.7 us; the launch traced here: 27.3 us
  Pallas kernels  26.7 us (96%)
  between operations  0.64 us (2%)
    pallas_call x1, Pallas kernels, shards(): pl.pallas_call(lambda *refs: exchange(n_gx, n_gy, *refs), out_shape=[pltp...  25.6 us
    pallas_call x1, Pallas kernels, shards(): pl.pallas_call(finish, out_shape=[jax.ShapeDtypeStruct((2, FIELDS, 256, L...  1.1 us

profile of v3, /device:TPU:1, one launch (start us, length us, event | category | flops | bytes accessed | tf_op | source)
XLA Modules:
  0.0 27.3 jit_solution(5142123481236555904)
XLA Ops:
  0.6 25.6 %shard_map.59 = (f32[2,5,256,128]{3,2,1,0:T(8,128)S(1)}, f32[2,5,256,128]{3,2,1,0:T(8,128)S(1)}, f32[5,3,8,128]{3,2,1,0:T(8,128)S(1)}, f32[2,2,5,8,128]{4,3,2,1,0:T(8,128)S(1)}, f32[5,16,128]{2,1,0:T(8,128)S(1)}) custom-call(s32[2,2,5]{2,1,0:T(2,128)} %refs_0_.1, f32[2,5,256,128]{3,2,1,0:T(8,128)} %bitcast.25, f32[2,5,16,128]{3,2,1,0:T(8,128)} %bitcast.26, ...), custom_call_target="tpu_custom_call" | custom-call | tf_op jit(solution)/shard_map/pallas_call | solution.py:411
  26.2 1.1 %shard_map.60 = (f32[2,5,256,128]{3,2,1,0:T(8,128)}, f32[5,16,128]{2,1,0:T(8,128)}) custom-call(f32[2,5,256,128]{3,2,1,0:T(8,128)S(1)} %get-tuple-element.9.done, f32[2,5,256,128]{3,2,1,0:T(8,128)S(1)} %get-tuple-element.10.cells, f32[5,3,8,128]{3,2,1,0:T(8,128)S(1)} %get-tuple-element.11.low_ghosts, f32[2,2,5,8,128]{4,3,2,1,0:T(8,128)S(1)} %get-tuple-element.12.kept, ...), custom_call_target="tpu_custom_call" | custom-call | tf_op jit(solution)/shard_map/pallas_call | solution.py:445

commit v4 on v3

--- a/solution.py
+++ b/solution.py
@@ -16,6 +16,10 @@
 
 def load_plane(ref, block, x):
     return [ref[block, f, plane_rows(x), :] for f in range(FIELDS)]
+
+
+def planes_of(ref, x):
+    return [ref[f, :, x, 0, :] for f in range(FIELDS)]
 
 
 def primitive(cell):
@@ -178,11 +182,11 @@
 
 
 def exchange(
-    n_gx, n_gy, links_in, fine, coarse, register,
+    n_gx, n_gy, links_in, fine, planes, coarse, register,
     out, cells, low_ghosts, kept, faces_out,
-    from_below, from_above, links, own_coarse, own_register, low_faces, high_faces, own_q,
-    coarse_below, coarse_above, low_below, high_above, q_below, q_above,
-    local_sem, send_sem, recv_sem, relay_sem, beside_sem,
+    from_below, from_above, links, own_coarse, own_register,
+    coarse_below, coarse_above, low_below, high_above, links_below, links_above,
+    local_sem, send_sem, recv_sem, relay_sem, beside_sem, below_sem,
 ):
     gx, gy = lax.axis_index("gx"), lax.axis_index("gy")
     above = (lax.rem(gx + 1, n_gx), gy)
@@ -197,17 +201,9 @@
         copy.start()
         return copy
 
-    def rows(ref, start, size):
-        return ref.at[:, :, pl.ds(start, size), :]
-
     def signal(semaphore, device):
         pl.semaphore_signal(semaphore, inc=1, device_id=device, device_id_type=MESH)
 
-    high_in = [
-        fetch(fine.at[b, :, pl.ds(192, 64), :], cells.at[b, :, pl.ds(192, 64), :], b)
-        for b in range(2)
-    ]
-
     barrier = pltpu.get_barrier_semaphore()
     signal(barrier, below)
 
@@ -216,13 +212,8 @@
         signal(barrier, right)
         signal(barrier, left)
 
-    low_in = fetch(rows(fine, 0, 64), rows(cells, 0, 64), 2)
-    links_in_copy = fetch(links_in, links, 3)
-    middle_in = fetch(rows(fine, 64, 128), rows(cells, 64, 128), 4)
-    coarse_in = fetch(coarse, own_coarse, 5)
-    register_in = fetch(register, own_register, 6)
-
     pl.semaphore_wait(barrier, jnp.where(is_last, 1, 3))
+    signal(below_sem, above)
 
     def remote(src, dst, device, k):
         return pltpu.make_async_remote_copy(
@@ -230,14 +221,20 @@
             device_id=device, device_id_type=MESH,
         )
 
-    coarse_up = remote(coarse.at[0], coarse_below, above, 0)
-    fine_up = [remote(high_faces.at[b], from_below.at[1, b], above, 1 + b) for b in range(2)]
-    low_up = remote(low_faces.at[0], low_below, above, 3)
-    q_up = remote(own_q.at[0], q_below, above, 4)
+    def high(b):
+        return planes.at[b, :, 3, :, pl.ds(5, 3)]
+
+    def low(b):
+        return planes.at[b, :, 0, :, pl.ds(0, 3)]
+
+    fine_up = [remote(high(b), from_below.at[1, b], above, b) for b in range(2)]
+    coarse_up = remote(coarse.at[0], coarse_below, above, 2)
+    low_up = remote(low(0), low_below, above, 3)
+    links_up = remote(links_in, links_below, above, 4)
     coarse_down = remote(coarse.at[1], coarse_above, below, 5)
-    fine_down = [remote(low_faces.at[b], from_above.at[1, b], below, 6 + b) for b in range(2)]
-    high_down = remote(high_faces.at[0], high_above, below, 8)
-    q_down = remote(own_q.at[1], q_above, below, 9)
+    fine_down = [remote(low(b), from_above.at[1, b], below, 6 + b) for b in range(2)]
+    high_down = remote(high(0), high_above, below, 8)
+    links_down = remote(links_in, links_above, below, 9)
     on_up, on_down = (
         [
             [
@@ -249,27 +246,20 @@
         for ref, base in ((from_below, 10), (from_above, 14))
     )
 
-    for b in range(2):
-        high_in[b].wait()
-        for f in range(FIELDS):
-            for x in range(3):
-                high_faces[b, f, x] = cells[b, f, plane_rows(29 + x), :]
-        fine_up[b].start()
-    low_in.wait()
-    for b in range(2):
-        for f in range(FIELDS):
-            for x in range(3):
-                low_faces[b, f, x] = cells[b, f, plane_rows(x), :]
-    links_in_copy.wait()
-    for side in range(2):
-        own_q[side] = jnp.full((ROWS, LANES), links[0, side, 4], jnp.int32)
-    middle_in.wait()
+    for copy in fine_up:
+        copy.start()
+    cells_in = [fetch(fine.at[b], cells.at[b], b) for b in range(2)]
+    links_copy = fetch(links_in, links, 2)
+    coarse_in = fetch(coarse, own_coarse, 3)
+    register_in = fetch(register, own_register, 4)
+    cells_in[0].wait()
     bulk(cells, out, kept, 0)
     for copy in fine_up:
         copy.wait_send()
     coarse_up.start()
     low_up.start()
-    q_up.start()
+    links_up.start()
+    cells_in[1].wait()
     bulk(cells, out, kept, 1)
 
     def forward(arriving, onward):
@@ -279,34 +269,29 @@
                 copy.start()
 
     def send_down():
-        for copy in [coarse_down] + fine_down + [high_down, q_down]:
+        for copy in [coarse_down] + fine_down + [high_down, links_down]:
             copy.start()
 
     @pl.when(is_first)
     def _():
         forward(fine_down, on_down)
 
-    fine_up[0].wait_recv()
-
-    @pl.when(jnp.logical_not(is_first))
-    def _():
-        send_down()
-
-    @pl.when(is_last)
-    def _():
-        pl.semaphore_wait(beside_sem, 1)
-
-    for copy in on_up[0]:
-        copy.start()
-    fine_up[1].wait_recv()
-    for copy in on_up[1]:
-        copy.start()
+    pl.semaphore_wait(below_sem, 1)
+    send_down()
 
     @pl.when(is_first)
     def _():
         signal(relay_sem.at[0], right)
         signal(relay_sem.at[1], left)
-        send_down()
+
+    @pl.when(is_last)
+    def _():
+        pl.semaphore_wait(beside_sem, 1)
+
+    forward(fine_up, on_up)
+
+    @pl.when(is_first)
+    def _():
         pl.semaphore_wait(relay_sem.at[0], 1)
         pl.semaphore_wait(relay_sem.at[1], 1)
         signal(beside_sem, below)
@@ -318,6 +303,7 @@
     def store(f, x, value):
         out[0, f, plane_rows(x), :] = value
 
+    links_copy.wait()
     coarse_down.wait_recv()
     coarse_up.wait_recv()
     for side in range(2):
@@ -335,19 +321,20 @@
         for copy in pair:
             copy.wait_recv()
     column, slot = links[1, 1, 2], links[1, 1, 3]
-    ghost_planes = [[from_above[column, slot, f, x] for f in range(FIELDS)] for x in range(3)]
+    ghost_planes = [planes_of(from_above.at[column, slot], x) for x in range(3)]
     block_one_edge(1, ghost_planes, cells, kept, store_one)
 
     coarse_in.wait()
     register_in.wait()
-    for copy in (high_down, q_down, low_up, q_up):
+    for copy in (high_down, links_down, low_up, links_up):
         copy.wait_recv()
     for t in range(2):
         side = 1 - t
-        q = q_below[...] if side == 0 else q_above[...]
-        planes = low_below if side == 0 else high_above
+        their_links = links_below if side == 0 else links_above
+        q = jnp.broadcast_to(their_links[0][side : side + 1, 4:5], (ROWS, LANES))
+        outer = low_below if side == 0 else high_above
         ghosts = coarse_ghosts(own_coarse.at[t], side, q)
-        w = [primitive([planes[f, x] for f in range(FIELDS)]) for x in range(3)]
+        w = [primitive(planes_of(outer, x)) for x in range(3)]
         flux = single_flux(ghosts + w if side == 0 else w + ghosts)
         factor = 0.05 if t == 0 else -0.05
         here = pl.ds(t, ROWS, stride=2)
@@ -356,7 +343,7 @@
                 own_register[f, here, :] + patch(flux[f], q)
             )
 
-    for copy in [coarse_up, low_up, q_up, coarse_down, high_down, q_down] + fine_down:
+    for copy in [coarse_up, low_up, links_up, coarse_down, high_down, links_down] + fine_down:
         copy.wait_send()
     for pair in on_down + on_up:
         for copy in pair:
@@ -366,9 +353,9 @@
         for copy in pair:
             copy.wait_recv()
     column, slot = links[1, 0, 2], links[1, 0, 3]
-    for f in range(FIELDS):
-        for x in range(3):
-            low_ghosts[f, x] = from_below[column, slot, f, x]
+    for x in range(3):
+        for f, value in enumerate(planes_of(from_below.at[column, slot], x)):
+            low_ghosts[f, x] = value
 
 
 def finish(done, cells, low_ghosts, kept, faces, out, faces_out, tile, sem):
@@ -400,12 +387,14 @@
     n_gx, n_gy = lax.axis_size("gx"), lax.axis_size("gy")
     f32 = jnp.float32
     fine = fine_state.reshape(2, FIELDS, 4, 8, 8, LANES).transpose(0, 1, 2, 4, 3, 5)
+    planes = fine.reshape(2, FIELDS, 4, 8, 8, 1, LANES)
     fine = fine.reshape(2, FIELDS, 256, LANES)
     coarse = coarse_edges.reshape(2, FIELDS, 2, 8, LANES).transpose(0, 1, 3, 2, 4)
     coarse = coarse.reshape(2, FIELDS, 16, LANES)
     register = flux_register.reshape(2, FIELDS, 8, LANES).transpose(1, 2, 0, 3)
     register = register.reshape(FIELDS, 16, LANES)
     plane = (ROWS, LANES)
+    outer = (FIELDS, ROWS, 3, 1, LANES)
     hbm = pl.BlockSpec(memory_space=pltpu.HBM)
     vmem = pl.BlockSpec(memory_space=pltpu.VMEM)
     held = pl.pallas_call(
@@ -417,31 +406,29 @@
             pltpu.VMEM((2, 2, FIELDS) + plane, f32),
             pltpu.VMEM((FIELDS, 16, LANES), f32),
         ],
-        in_specs=[hbm] * 4,
+        in_specs=[hbm] * 5,
         out_specs=[vmem] * 5,
         scratch_shapes=[
-            pltpu.VMEM((3, 2, FIELDS, 3) + plane, f32),
-            pltpu.VMEM((3, 2, FIELDS, 3) + plane, f32),
+            pltpu.VMEM((3, 2) + outer, f32),
+            pltpu.VMEM((3, 2) + outer, f32),
             pltpu.SMEM((2, 2, 5), jnp.int32),
             pltpu.VMEM((2, FIELDS, 16, LANES), f32),
             pltpu.VMEM((FIELDS, 16, LANES), f32),
-            pltpu.VMEM((2, FIELDS, 3) + plane, f32),
-            pltpu.VMEM((2, FIELDS, 3) + plane, f32),
-            pltpu.VMEM((2,) + plane, jnp.int32),
             pltpu.VMEM((FIELDS, 16, LANES), f32),
             pltpu.VMEM((FIELDS, 16, LANES), f32),
-            pltpu.VMEM((FIELDS, 3) + plane, f32),
-            pltpu.VMEM((FIELDS, 3) + plane, f32),
-            pltpu.VMEM(plane, jnp.int32),
-            pltpu.VMEM(plane, jnp.int32),
-            pltpu.SemaphoreType.DMA((7,)),
+            pltpu.VMEM(outer, f32),
+            pltpu.VMEM(outer, f32),
+            pltpu.VMEM((2, 2, 5), jnp.int32),
+            pltpu.VMEM((2, 2, 5), jnp.int32),
+            pltpu.SemaphoreType.DMA((5,)),
             pltpu.SemaphoreType.DMA((18,)),
             pltpu.SemaphoreType.DMA((18,)),
             pltpu.SemaphoreType.REGULAR((2,)),
             pltpu.SemaphoreType.REGULAR,
+            pltpu.SemaphoreType.REGULAR,
         ],
         compiler_params=pltpu.CompilerParams(collective_id=0, has_side_effects=True),
-    )(fine_links, fine, coarse, register)
+    )(fine_links, fine, planes, coarse, register)
     updated, faces = pl.pallas_call(
         finish,
         out_shape=[

time: 27.7 us -> 26.8 us (0.968)
  Pallas kernels: 26.7 us -> 26 us
    pallas_call x1, Pallas kernels: 25.6 us -> 24.9 us  [shards(): pl.pallas_call(lambda *refs: exchange(n_gx, n_gy, *refs), out_shape=[pltp...]
where the time goes in v4:
time: 26.8 us; the launch traced here: 26.7 us
  Pallas kernels  26 us (97%)
  between operations  0.64 us (2%)
    pallas_call x1, Pallas kernels, shards(): pl.pallas_call(lambda *refs: exchange(n_gx, n_gy, *refs), out_shape=[pltp...  24.9 us
    pallas_call x1, Pallas kernels, shards(): pl.pallas_call(finish, out_shape=[jax.ShapeDtypeStruct((2, FIELDS, 256, L...  1.1 us

profile of v4, /device:TPU:1, one launch (start us, length us, event | category | flops | bytes accessed | tf_op | source)
XLA Modules:
  0.0 26.7 jit_solution(18004236911479906720)
XLA Ops:
  0.6 24.9 %shard_map.59 = (f32[2,5,256,128]{3,2,1,0:T(8,128)S(1)}, f32[2,5,256,128]{3,2,1,0:T(8,128)S(1)}, f32[5,3,8,128]{3,2,1,0:T(8,128)S(1)}, f32[2,2,5,8,128]{4,3,2,1,0:T(8,128)S(1)}, f32[5,16,128]{2,1,0:T(8,128)S(1)}) custom-call(s32[2,2,5]{2,1,0:T(2,128)} %refs_0_.1, f32[2,5,256,128]{3,2,1,0:T(8,128)} %bitcast.27, f32[2,5,4,8,8,1,128]{6,5,4,3,2,1,0:T(1,128)} %bitcast.28, ...), custom_call_target="tpu_custom_call" | custom-call | tf_op jit(solution)/shard_map/pallas_call | solution.py:400
  25.6 1.1 %shard_map.60 = (f32[2,5,256,128]{3,2,1,0:T(8,128)}, f32[5,16,128]{2,1,0:T(8,128)}) custom-call(f32[2,5,256,128]{3,2,1,0:T(8,128)S(1)} %get-tuple-element.9.done, f32[2,5,256,128]{3,2,1,0:T(8,128)S(1)} %get-tuple-element.10.cells, f32[5,3,8,128]{3,2,1,0:T(8,128)S(1)} %get-tuple-element.11.low_ghosts, f32[2,2,5,8,128]{4,3,2,1,0:T(8,128)S(1)} %get-tuple-element.12.kept, ...), custom_call_target="tpu_custom_call" | custom-call | tf_op jit(solution)/shard_map/pallas_call | solution.py:432

commit v5 on v4

--- a/solution.py
+++ b/solution.py
@@ -193,6 +193,7 @@
     below = (lax.rem(gx + n_gx - 1, n_gx), gy)
     right = (gx, lax.rem(gy + 1, n_gy))
     left = (gx, lax.rem(gy + n_gy - 1, n_gy))
+    odd = lax.rem(gy, 2) == 1
     is_first = gx == 0
     is_last = gx == n_gx - 1
 
@@ -207,12 +208,16 @@
     barrier = pltpu.get_barrier_semaphore()
     signal(barrier, below)
 
+    @pl.when(odd)
+    def _():
+        signal(barrier, (below[0], right[1]))
+
     @pl.when(jnp.logical_not(is_last))
     def _():
         signal(barrier, right)
         signal(barrier, left)
 
-    pl.semaphore_wait(barrier, jnp.where(is_last, 1, 3))
+    pl.semaphore_wait(barrier, jnp.where(is_last, 1, 3) + jnp.where(odd, 0, 1))
     signal(below_sem, above)
 
     def remote(src, dst, device, k):
@@ -232,22 +237,29 @@
     low_up = remote(low(0), low_below, above, 3)
     links_up = remote(links_in, links_below, above, 4)
     coarse_down = remote(coarse.at[1], coarse_above, below, 5)
-    fine_down = [remote(low(b), from_above.at[1, b], below, 6 + b) for b in range(2)]
-    high_down = remote(high(0), high_above, below, 8)
-    links_down = remote(links_in, links_above, below, 9)
-    on_up, on_down = (
+    fine_down = remote(planes.at[:, :, 0, :, pl.ds(0, 3)], from_above.at[1], below, 6)
+    high_down = remote(high(0), high_above, below, 7)
+    links_down = remote(links_in, links_above, below, 8)
+    across_up = remote(high(1), from_below.at[2, 1], (above[0], left[1]), 12)
+    on_up = [
         [
-            [
-                remote(ref.at[1, b], ref.at[0, b], right, base + 2 * b),
-                remote(ref.at[1, b], ref.at[2, b], left, base + 2 * b + 1),
-            ]
-            for b in range(2)
+            remote(from_below.at[1, b], from_below.at[0, b], right, 9 + 2 * b),
+            remote(from_below.at[1, b], from_below.at[2, b], left, 10 + 2 * b),
         ]
-        for ref, base in ((from_below, 10), (from_above, 14))
-    )
-
-    for copy in fine_up:
-        copy.start()
+        for b in range(2)
+    ]
+    on_down = [
+        remote(from_above.at[1], from_above.at[0], right, 13),
+        remote(from_above.at[1], from_above.at[2], left, 14),
+    ]
+
+    fine_up[0].start()
+    fine_up[1].start()
+
+    @pl.when(jnp.logical_not(odd))
+    def _():
+        across_up.start()
+
     cells_in = [fetch(fine.at[b], cells.at[b], b) for b in range(2)]
     links_copy = fetch(links_in, links, 2)
     coarse_in = fetch(coarse, own_coarse, 3)
@@ -262,19 +274,18 @@
     cells_in[1].wait()
     bulk(cells, out, kept, 1)
 
-    def forward(arriving, onward):
-        for b in range(2):
-            arriving[b].wait_recv()
-            for copy in onward[b]:
-                copy.start()
+    def forward_down():
+        fine_down.wait_recv()
+        for copy in on_down:
+            copy.start()
 
     def send_down():
-        for copy in [coarse_down] + fine_down + [high_down, links_down]:
+        for copy in (coarse_down, fine_down, high_down, links_down):
             copy.start()
 
     @pl.when(is_first)
     def _():
-        forward(fine_down, on_down)
+        forward_down()
 
     pl.semaphore_wait(below_sem, 1)
     send_down()
@@ -288,7 +299,16 @@
     def _():
         pl.semaphore_wait(beside_sem, 1)
 
-    forward(fine_up, on_up)
+    fine_up[0].wait_recv()
+    for copy in on_up[0]:
+        copy.start()
+    fine_up[1].wait_recv()
+    on_up[1][0].start()
+
+    @pl.when(odd)
+    def _():
+        on_up[1][1].start()
+
 
     @pl.when(is_first)
     def _():
@@ -298,15 +318,12 @@
 
     @pl.when(jnp.logical_not(is_first))
     def _():
-        forward(fine_down, on_down)
+        forward_down()
 
     def store(f, x, value):
         out[0, f, plane_rows(x), :] = value
 
-    links_copy.wait()
-    coarse_down.wait_recv()
-    coarse_up.wait_recv()
-    for side in range(2):
+    def block_zero_edge(side):
         ghosts = coarse_ghosts(coarse_above if side == 0 else coarse_below, side, links[0, side, 4])
         _, third = edge_planes(cells, 0, side, ghosts, store)
         x = 2 if side == 0 else 29
@@ -314,21 +331,7 @@
             change = kept[0, 0, f] - third[f] if side == 0 else third[f] - kept[0, 1, f]
             store(f, x, cells[0, f, plane_rows(x), :] - 0.1 * change)
 
-    def store_one(f, x, value):
-        out[1, f, plane_rows(x), :] = value
-
-    for pair in on_down:
-        for copy in pair:
-            copy.wait_recv()
-    column, slot = links[1, 1, 2], links[1, 1, 3]
-    ghost_planes = [planes_of(from_above.at[column, slot], x) for x in range(3)]
-    block_one_edge(1, ghost_planes, cells, kept, store_one)
-
-    coarse_in.wait()
-    register_in.wait()
-    for copy in (high_down, links_down, low_up, links_up):
-        copy.wait_recv()
-    for t in range(2):
+    def coarse_face(t):
         side = 1 - t
         their_links = links_below if side == 0 else links_above
         q = jnp.broadcast_to(their_links[0][side : side + 1, 4:5], (ROWS, LANES))
@@ -343,15 +346,35 @@
                 own_register[f, here, :] + patch(flux[f], q)
             )
 
-    for copy in [coarse_up, low_up, links_up, coarse_down, high_down, links_down] + fine_down:
+    def store_one(f, x, value):
+        out[1, f, plane_rows(x), :] = value
+
+    links_copy.wait()
+    coarse_in.wait()
+    register_in.wait()
+    coarse_down.wait_recv()
+    block_zero_edge(0)
+    for copy in (high_down, links_down):
+        copy.wait_recv()
+    coarse_face(0)
+    for copy in on_down:
+        copy.wait_recv()
+    column, slot = links[1, 1, 2], links[1, 1, 3]
+    ghost_planes = [planes_of(from_above.at[column, slot], x) for x in range(3)]
+    block_one_edge(1, ghost_planes, cells, kept, store_one)
+    coarse_up.wait_recv()
+    block_zero_edge(1)
+    for copy in (low_up, links_up):
+        copy.wait_recv()
+    coarse_face(1)
+
+    for copy in (coarse_up, low_up, links_up, coarse_down, fine_down, high_down, links_down):
         copy.wait_send()
-    for pair in on_down + on_up:
-        for copy in pair:
-            copy.wait_send()
-
-    for pair in on_up:
-        for copy in pair:
-            copy.wait_recv()
+    for copy in on_down + on_up[0] + on_up[1]:
+        copy.wait_send()
+
+    for copy in on_up[0] + on_up[1]:
+        copy.wait_recv()
     column, slot = links[1, 0, 2], links[1, 0, 3]
     for x in range(3):
         for f, value in enumerate(planes_of(from_below.at[column, slot], x)):
@@ -421,8 +444,8 @@
             pltpu.VMEM((2, 2, 5), jnp.int32),
             pltpu.VMEM((2, 2, 5), jnp.int32),
             pltpu.SemaphoreType.DMA((5,)),
-            pltpu.SemaphoreType.DMA((18,)),
-            pltpu.SemaphoreType.DMA((18,)),
+            pltpu.SemaphoreType.DMA((15,)),
+            pltpu.SemaphoreType.DMA((15,)),
             pltpu.SemaphoreType.REGULAR((2,)),
             pltpu.SemaphoreType.REGULAR,
             pltpu.SemaphoreType.REGULAR,

time: 26.8 us -> 26.3 us (0.981)
  Pallas kernels: 26 us -> 25.5 us
    pallas_call x1, Pallas kernels: 24.9 us -> 24.4 us  [shards(): pl.pallas_call(lambda *refs: exchange(n_gx, n_gy, *refs), out_shape=[pltp...]
where the time goes in v5:
time: 26.3 us; the launch traced here: 26.1 us
  Pallas kernels  25.5 us (97%)
  between operations  0.64 us (2%)
    pallas_call x1, Pallas kernels, shards(): pl.pallas_call(lambda *refs: exchange(n_gx, n_gy, *refs), out_shape=[pltp...  24.4 us
    pallas_call x1, Pallas kernels, shards(): pl.pallas_call(finish, out_shape=[jax.ShapeDtypeStruct((2, FIELDS, 256, L...  1.1 us

profile of v5, /device:TPU:1, one launch (start us, length us, event | category | flops | bytes accessed | tf_op | source)
XLA Modules:
  0.0 26.1 jit_solution(17636925383572489084)
XLA Ops:
  0.6 24.4 %shard_map.59 = (f32[2,5,256,128]{3,2,1,0:T(8,128)S(1)}, f32[2,5,256,128]{3,2,1,0:T(8,128)S(1)}, f32[5,3,8,128]{3,2,1,0:T(8,128)S(1)}, f32[2,2,5,8,128]{4,3,2,1,0:T(8,128)S(1)}, f32[5,16,128]{2,1,0:T(8,128)S(1)}) custom-call(s32[2,2,5]{2,1,0:T(2,128)} %refs_0_.1, f32[2,5,256,128]{3,2,1,0:T(8,128)} %bitcast.27, f32[2,5,4,8,8,1,128]{6,5,4,3,2,1,0:T(1,128)} %bitcast.28, ...), custom_call_target="tpu_custom_call" | custom-call | tf_op jit(solution)/shard_map/pallas_call | solution.py:423
  25.0 1.1 %shard_map.60 = (f32[2,5,256,128]{3,2,1,0:T(8,128)}, f32[5,16,128]{2,1,0:T(8,128)}) custom-call(f32[2,5,256,128]{3,2,1,0:T(8,128)S(1)} %get-tuple-element.9.done, f32[2,5,256,128]{3,2,1,0:T(8,128)S(1)} %get-tuple-element.10.cells, f32[5,3,8,128]{3,2,1,0:T(8,128)S(1)} %get-tuple-element.11.low_ghosts, f32[2,2,5,8,128]{4,3,2,1,0:T(8,128)S(1)} %get-tuple-element.12.kept, ...), custom_call_target="tpu_custom_call" | custom-call | tf_op jit(solution)/shard_map/pallas_call | solution.py:455

commit v6 on v5

--- a/solution.py
+++ b/solution.py
@@ -218,7 +218,6 @@
         signal(barrier, left)
 
     pl.semaphore_wait(barrier, jnp.where(is_last, 1, 3) + jnp.where(odd, 0, 1))
-    signal(below_sem, above)
 
     def remote(src, dst, device, k):
         return pltpu.make_async_remote_copy(
@@ -232,7 +231,16 @@
     def low(b):
         return planes.at[b, :, 0, :, pl.ds(0, 3)]
 
-    fine_up = [remote(high(b), from_below.at[1, b], above, b) for b in range(2)]
+    parts = [(0, pl.ds(0, 3)), (0, pl.ds(3, 2)), (1, pl.ds(0, 5))]
+
+    def part(index, column):
+        b, fields = parts[index]
+        return from_below.at[column, b, fields]
+
+    fine_up = [
+        remote(planes.at[b, fields, 3, :, pl.ds(5, 3)], part(k, 1), above, (0, 1, 15)[k])
+        for k, (b, fields) in enumerate(parts)
+    ]
     coarse_up = remote(coarse.at[0], coarse_below, above, 2)
     low_up = remote(low(0), low_below, above, 3)
     links_up = remote(links_in, links_below, above, 4)
@@ -242,24 +250,22 @@
     links_down = remote(links_in, links_above, below, 8)
     across_up = remote(high(1), from_below.at[2, 1], (above[0], left[1]), 12)
     on_up = [
-        [
-            remote(from_below.at[1, b], from_below.at[0, b], right, 9 + 2 * b),
-            remote(from_below.at[1, b], from_below.at[2, b], left, 10 + 2 * b),
-        ]
-        for b in range(2)
+        [remote(part(k, 1), part(k, 0), right, r), remote(part(k, 1), part(k, 2), left, l)]
+        for k, (r, l) in enumerate(((9, 10), (16, 17), (11, 12)))
     ]
     on_down = [
         remote(from_above.at[1], from_above.at[0], right, 13),
         remote(from_above.at[1], from_above.at[2], left, 14),
     ]
 
-    fine_up[0].start()
-    fine_up[1].start()
+    for copy in fine_up:
+        copy.start()
 
     @pl.when(jnp.logical_not(odd))
     def _():
         across_up.start()
 
+    signal(below_sem, above)
     cells_in = [fetch(fine.at[b], cells.at[b], b) for b in range(2)]
     links_copy = fetch(links_in, links, 2)
     coarse_in = fetch(coarse, own_coarse, 3)
@@ -299,15 +305,16 @@
     def _():
         pl.semaphore_wait(beside_sem, 1)
 
-    fine_up[0].wait_recv()
-    for copy in on_up[0]:
-        copy.start()
-    fine_up[1].wait_recv()
-    on_up[1][0].start()
+    for k in range(2):
+        fine_up[k].wait_recv()
+        for copy in on_up[k]:
+            copy.start()
+    fine_up[2].wait_recv()
+    on_up[2][0].start()
 
     @pl.when(odd)
     def _():
-        on_up[1][1].start()
+        on_up[2][1].start()
 
 
     @pl.when(is_first)
@@ -370,10 +377,10 @@
 
     for copy in (coarse_up, low_up, links_up, coarse_down, fine_down, high_down, links_down):
         copy.wait_send()
-    for copy in on_down + on_up[0] + on_up[1]:
+    for copy in on_down + on_up[0] + on_up[1] + on_up[2]:
         copy.wait_send()
 
-    for copy in on_up[0] + on_up[1]:
+    for copy in on_up[0] + on_up[1] + on_up[2]:
         copy.wait_recv()
     column, slot = links[1, 0, 2], links[1, 0, 3]
     for x in range(3):
@@ -444,8 +451,8 @@
             pltpu.VMEM((2, 2, 5), jnp.int32),
             pltpu.VMEM((2, 2, 5), jnp.int32),
             pltpu.SemaphoreType.DMA((5,)),
-            pltpu.SemaphoreType.DMA((15,)),
-            pltpu.SemaphoreType.DMA((15,)),
+            pltpu.SemaphoreType.DMA((18,)),
+            pltpu.SemaphoreType.DMA((18,)),
             pltpu.SemaphoreType.REGULAR((2,)),
             pltpu.SemaphoreType.REGULAR,
             pltpu.SemaphoreType.REGULAR,

time: 26.3 us -> 26.1 us (level)
  no operation moved by 1% of the time
where the time goes in v6:
time: 26.1 us; the launch traced here: 25.9 us
  Pallas kernels  25.3 us (97%)
  between operations  0.64 us (2%)
    pallas_call x1, Pallas kernels, shards(): pl.pallas_call(lambda *refs: exchange(n_gx, n_gy, *refs), out_shape=[pltp...  24.2 us
    pallas_call x1, Pallas kernels, shards(): pl.pallas_call(finish, out_shape=[jax.ShapeDtypeStruct((2, FIELDS, 256, L...  1.1 us

profile of v6, /device:TPU:1, one launch (start us, length us, event | category | flops | bytes accessed | tf_op | source)
XLA Modules:
  0.0 25.9 jit_solution(11381423057418569922)
XLA Ops:
  0.6 24.2 %shard_map.59 = (f32[2,5,256,128]{3,2,1,0:T(8,128)S(1)}, f32[2,5,256,128]{3,2,1,0:T(8,128)S(1)}, f32[5,3,8,128]{3,2,1,0:T(8,128)S(1)}, f32[2,2,5,8,128]{4,3,2,1,0:T(8,128)S(1)}, f32[5,16,128]{2,1,0:T(8,128)S(1)}) custom-call(s32[2,2,5]{2,1,0:T(2,128)} %refs_0_.1, f32[2,5,256,128]{3,2,1,0:T(8,128)} %bitcast.27, f32[2,5,4,8,8,1,128]{6,5,4,3,2,1,0:T(1,128)} %bitcast.28, ...), custom_call_target="tpu_custom_call" | custom-call | tf_op jit(solution)/shard_map/pallas_call | solution.py:430
  24.8 1.1 %shard_map.60 = (f32[2,5,256,128]{3,2,1,0:T(8,128)}, f32[5,16,128]{2,1,0:T(8,128)}) custom-call(f32[2,5,256,128]{3,2,1,0:T(8,128)S(1)} %get-tuple-element.9.done, f32[2,5,256,128]{3,2,1,0:T(8,128)S(1)} %get-tuple-element.10.cells, f32[5,3,8,128]{3,2,1,0:T(8,128)S(1)} %get-tuple-element.11.low_ghosts, f32[2,2,5,8,128]{4,3,2,1,0:T(8,128)S(1)} %get-tuple-element.12.kept, ...), custom_call_target="tpu_custom_call" | custom-call | tf_op jit(solution)/shard_map/pallas_call | solution.py:462

commit v7 on v6

--- a/solution.py
+++ b/solution.py
@@ -307,8 +307,8 @@
 
     for k in range(2):
         fine_up[k].wait_recv()
-        for copy in on_up[k]:
-            copy.start()
+        on_up[k][1].start()
+        on_up[k][0].start()
     fine_up[2].wait_recv()
     on_up[2][0].start()
 

time: 26.1 us -> 26.1 us (level)
  no operation moved by 1% of the time
where the time goes in v7:
time: 26.1 us; the launch traced here: 25.9 us
  Pallas kernels  25.3 us (97%)
  between operations  0.64 us (2%)
    pallas_call x1, Pallas kernels, shards(): pl.pallas_call(lambda *refs: exchange(n_gx, n_gy, *refs), out_shape=[pltp...  24.2 us
    pallas_call x1, Pallas kernels, shards(): pl.pallas_call(finish, out_shape=[jax.ShapeDtypeStruct((2, FIELDS, 256, L...  1.1 us

profile of v7, /device:TPU:1, one launch (start us, length us, event | category | flops | bytes accessed | tf_op | source)
XLA Modules:
  0.0 25.9 jit_solution(484428618702598231)
XLA Ops:
  0.6 24.2 %shard_map.59 = (f32[2,5,256,128]{3,2,1,0:T(8,128)S(1)}, f32[2,5,256,128]{3,2,1,0:T(8,128)S(1)}, f32[5,3,8,128]{3,2,1,0:T(8,128)S(1)}, f32[2,2,5,8,128]{4,3,2,1,0:T(8,128)S(1)}, f32[5,16,128]{2,1,0:T(8,128)S(1)}) custom-call(s32[2,2,5]{2,1,0:T(2,128)} %refs_0_.1, f32[2,5,256,128]{3,2,1,0:T(8,128)} %bitcast.27, f32[2,5,4,8,8,1,128]{6,5,4,3,2,1,0:T(1,128)} %bitcast.28, ...), custom_call_target="tpu_custom_call" | custom-call | tf_op jit(solution)/shard_map/pallas_call | solution.py:430
  24.8 1.1 %shard_map.60 = (f32[2,5,256,128]{3,2,1,0:T(8,128)}, f32[5,16,128]{2,1,0:T(8,128)}) custom-call(f32[2,5,256,128]{3,2,1,0:T(8,128)S(1)} %get-tuple-element.9.done, f32[2,5,256,128]{3,2,1,0:T(8,128)S(1)} %get-tuple-element.10.cells, f32[5,3,8,128]{3,2,1,0:T(8,128)S(1)} %get-tuple-element.11.low_ghosts, f32[2,2,5,8,128]{4,3,2,1,0:T(8,128)S(1)} %get-tuple-element.12.kept, ...), custom_call_target="tpu_custom_call" | custom-call | tf_op jit(solution)/shard_map/pallas_call | solution.py:462

commit v8 on v7

--- a/solution.py
+++ b/solution.py
@@ -219,10 +219,10 @@
 
     pl.semaphore_wait(barrier, jnp.where(is_last, 1, 3) + jnp.where(odd, 0, 1))
 
-    def remote(src, dst, device, k):
+    def remote(src, dst, device, k, k_send=None):
         return pltpu.make_async_remote_copy(
-            src_ref=src, dst_ref=dst, send_sem=send_sem.at[k], recv_sem=recv_sem.at[k],
-            device_id=device, device_id_type=MESH,
+            src_ref=src, dst_ref=dst, send_sem=send_sem.at[k if k_send is None else k_send],
+            recv_sem=recv_sem.at[k], device_id=device, device_id_type=MESH,
         )
 
     def high(b):
@@ -238,20 +238,20 @@
         return from_below.at[column, b, fields]
 
     fine_up = [
-        remote(planes.at[b, fields, 3, :, pl.ds(5, 3)], part(k, 1), above, (0, 1, 15)[k])
+        remote(planes.at[b, fields, 3, :, pl.ds(5, 3)], part(k, 1), above, (0, 1, 15)[k], (0, 1, 4)[k])
         for k, (b, fields) in enumerate(parts)
     ]
-    coarse_up = remote(coarse.at[0], coarse_below, above, 2)
-    low_up = remote(low(0), low_below, above, 3)
-    links_up = remote(links_in, links_below, above, 4)
+    coarse_up = remote(coarse.at[0], coarse_below, above, 2, 0)
+    low_up = remote(low(0), low_below, above, 3, 1)
+    links_up = remote(links_in, links_below, above, 4, 4)
     coarse_down = remote(coarse.at[1], coarse_above, below, 5)
     fine_down = remote(planes.at[:, :, 0, :, pl.ds(0, 3)], from_above.at[1], below, 6)
     high_down = remote(high(0), high_above, below, 7)
     links_down = remote(links_in, links_above, below, 8)
     across_up = remote(high(1), from_below.at[2, 1], (above[0], left[1]), 12)
     on_up = [
-        [remote(part(k, 1), part(k, 0), right, r), remote(part(k, 1), part(k, 2), left, l)]
-        for k, (r, l) in enumerate(((9, 10), (16, 17), (11, 12)))
+        [remote(part(k, 1), part(k, 0), right, r, a), remote(part(k, 1), part(k, 2), left, l, b)]
+        for k, (r, l, a, b) in enumerate(((9, 10, 9, 10), (16, 17, 2, 3), (11, 12, 11, 12)))
     ]
     on_down = [
         remote(from_above.at[1], from_above.at[0], right, 13),
@@ -451,7 +451,7 @@
             pltpu.VMEM((2, 2, 5), jnp.int32),
             pltpu.VMEM((2, 2, 5), jnp.int32),
             pltpu.SemaphoreType.DMA((5,)),
-            pltpu.SemaphoreType.DMA((18,)),
+            pltpu.SemaphoreType.DMA((15,)),
             pltpu.SemaphoreType.DMA((18,)),
             pltpu.SemaphoreType.REGULAR((2,)),
             pltpu.SemaphoreType.REGULAR,

time: 26.1 us -> 26 us (level)
  no operation moved by 1% of the time
where the time goes in v8:
time: 26 us; the launch traced here: 25.9 us
  Pallas kernels  25.2 us (97%)
  between operations  0.64 us (2%)
    pallas_call x1, Pallas kernels, shards(): pl.pallas_call(lambda *refs: exchange(n_gx, n_gy, *refs), out_shape=[pltp...  24.1 us
    pallas_call x1, Pallas kernels, shards(): pl.pallas_call(finish, out_shape=[jax.ShapeDtypeStruct((2, FIELDS, 256, L...  1.1 us

profile of v8, /device:TPU:1, one launch (start us, length us, event | category | flops | bytes accessed | tf_op | source)
XLA Modules:
  0.0 25.9 jit_solution(11055579504457960675)
XLA Ops:
  0.6 24.1 %shard_map.59 = (f32[2,5,256,128]{3,2,1,0:T(8,128)S(1)}, f32[2,5,256,128]{3,2,1,0:T(8,128)S(1)}, f32[5,3,8,128]{3,2,1,0:T(8,128)S(1)}, f32[2,2,5,8,128]{4,3,2,1,0:T(8,128)S(1)}, f32[5,16,128]{2,1,0:T(8,128)S(1)}) custom-call(s32[2,2,5]{2,1,0:T(2,128)} %refs_0_.1, f32[2,5,256,128]{3,2,1,0:T(8,128)} %bitcast.27, f32[2,5,4,8,8,1,128]{6,5,4,3,2,1,0:T(1,128)} %bitcast.28, ...), custom_call_target="tpu_custom_call" | custom-call | tf_op jit(solution)/shard_map/pallas_call | solution.py:430
  24.8 1.1 %shard_map.60 = (f32[2,5,256,128]{3,2,1,0:T(8,128)}, f32[5,16,128]{2,1,0:T(8,128)}) custom-call(f32[2,5,256,128]{3,2,1,0:T(8,128)S(1)} %get-tuple-element.9.done, f32[2,5,256,128]{3,2,1,0:T(8,128)S(1)} %get-tuple-element.10.cells, f32[5,3,8,128]{3,2,1,0:T(8,128)S(1)} %get-tuple-element.11.low_ghosts, f32[2,2,5,8,128]{4,3,2,1,0:T(8,128)S(1)} %get-tuple-element.12.kept, ...), custom_call_target="tpu_custom_call" | custom-call | tf_op jit(solution)/shard_map/pallas_call | solution.py:462
